TPU v7x, 32 devices: a whole 2x2x4 slice. The times are simulated.
32 devices in a mesh: grp: 4 (over y, core), sub: 8 (over z, x).
Axes of the slice: x: 2, y: 2, z: 4, core: 2. Of those that a mesh axis runs over, the one named last changes fastest.
Arguments:
- cluster_pos: float32 [3, 1024], P(None, 'sub'), may hold values from -3 to 3
- cluster_vel: float32 [3, 1024], P(None, 'sub'), may hold values from -15 to 15
- cluster_mass: float32 [1024], P('sub'), may hold values from 3 to 60
- galaxy_pos: float32 [3, 16384], P(None, ('grp', 'sub')), may hold values from -1 to 7
- galaxy_vel: float32 [3, 16384], P(None, ('grp', 'sub')), may hold values from -3 to 3
- galaxy_kind: int32 [16384], P(('grp', 'sub')), may hold values from 0 to 3
- species_mass: float32 [4], replicated, may hold values from 10 to 80
Outputs:
- cluster_pos_out: float32 [3, 1024], P(None, 'sub')
- cluster_vel_out: float32 [3, 1024], P(None, 'sub')
- galaxy_pos_out: float32 [3, 16384], P(None, ('grp', 'sub'))
- galaxy_vel_out: float32 [3, 16384], P(None, ('grp', 'sub'))
All inputs are finite; a program needn't handle non-finite values.
Results may differ from a plain program's by a relative error of at most 0.0003.
Values sent between devices are 32-bit elements; how exact they have to be, the bound alone decides.
No kernel may reach another device: no remote copies, remote signals or barrier semaphores. Data moves between devices by JAX's collectives and lax.ppermute only.
A program may use at most 64 MiB of HBM per device.

v0:
```python
import jax
import jax.numpy as jnp
from jax import lax
from jax.sharding import PartitionSpec as P

SUBSTEPS = 8


step_time = 0.5
bridge_soft = 0.01
cluster_soft = 0.0025
tile_limit = 524288


def pick_block(target_count, source_count):
    tile_size = target_count
    while tile_size > 1 and (
        tile_size * source_count > tile_limit or target_count % tile_size != 0
    ):
        tile_size = tile_size // 2
    return tile_size


def field(targets, sources, masses, soften):
    target_count = targets.shape[1]
    tile_size = pick_block(target_count, sources.shape[1])

    def field_one_tile(target_tile):
        separation = sources[:, None, :] - target_tile[:, :, None]
        distance = jnp.sum(separation * separation, axis=0) + soften
        inverse = lax.rsqrt(distance)
        weight = masses[None, :] * inverse * inverse * inverse
        return jnp.sum(separation * weight[None], axis=2)

    stacked = targets.reshape(3, target_count // tile_size, tile_size).transpose(1, 0, 2)
    result = lax.map(field_one_tile, stacked)
    return result.transpose(1, 0, 2).reshape(3, target_count)


def rates(target_pos, target_vel, source_pos, source_vel, masses, soften):
    target_count = target_pos.shape[1]
    tile_size = pick_block(target_count, source_pos.shape[1])

    def rates_one_tile(target_tile):
        separation = source_pos[:, None, :] - target_tile[:3, :, None]
        closing = source_vel[:, None, :] - target_tile[3:, :, None]
        distance = jnp.sum(separation * separation, axis=0) + soften
        inverse = lax.rsqrt(distance)
        weight = masses[None, :] * inverse * inverse * inverse
        radial = 3.0 * jnp.sum(separation * closing, axis=0) / distance
        acceleration = jnp.sum(separation * weight[None], axis=2)
        jerk_rate = jnp.sum((closing - radial[None] * separation) * weight[None], axis=2)
        return jnp.concatenate([acceleration, jerk_rate], axis=0)

    stacked = jnp.concatenate([target_pos, target_vel], axis=0)
    stacked = stacked.reshape(6, target_count // tile_size, tile_size).transpose(1, 0, 2)
    result = lax.map(rates_one_tile, stacked)
    return result.transpose(1, 0, 2).reshape(6, target_count)


def local(
    cluster_pos, cluster_vel, cluster_mass, galaxy_pos, galaxy_vel, galaxy_kind, species_mass
):
    star_count = cluster_pos.shape[1]
    member_count = lax.axis_size("sub")
    group_count = lax.axis_size("grp")
    total_stars = star_count * member_count
    total_bodies = galaxy_pos.shape[1] * member_count * group_count
    star_mass = cluster_mass / total_stars
    species = jnp.arange(species_mass.shape[0], dtype=jnp.int32)
    body_mass = (
        jnp.sum(
            jnp.where(galaxy_kind[None, :] == species[:, None], species_mass[:, None], 0.0), axis=0
        )
        / total_bodies
    )
    half_step = step_time / 2.0

    def kick(star_positions, body_positions):
        stacked = jnp.concatenate([star_positions, star_mass[None, :]], axis=0)
        gathered = lax.all_gather(stacked, "sub", axis=1, tiled=True)
        galaxy_push = field(body_positions, gathered[:3], gathered[3], bridge_soft)
        partial_value = field(gathered[:3], body_positions, body_mass, bridge_soft)
        summed = lax.psum(partial_value, ("grp", "sub"))
        cluster_pull = lax.dynamic_slice_in_dim(
            summed, lax.axis_index("sub") * star_count, star_count, 1
        )
        return (cluster_pull, galaxy_push)

    def evaluate(guess_pos, guess_vel):
        sources = jnp.concatenate([guess_pos, guess_vel, star_mass[None, :]], axis=0)
        target_pos, target_vel = (guess_pos, guess_vel)
        source_piece = lax.all_gather(sources, "sub", axis=1, tiled=True)
        result = rates(
            target_pos,
            target_vel,
            source_piece[:3],
            source_piece[3:6],
            source_piece[6],
            cluster_soft,
        )
        return (result[:3], result[3:])

    first_pull, first_push = kick(cluster_pos, galaxy_pos)
    star_vel = cluster_vel + half_step * first_pull
    body_vel = galaxy_vel + half_step * first_push
    body_pos = galaxy_pos + step_time * body_vel
    substep_time = step_time / SUBSTEPS
    positions, velocity = (cluster_pos, star_vel)
    acceleration, jerk_rate = evaluate(positions, velocity)
    for substep in range(SUBSTEPS):
        guess_pos = positions + substep_time * (
            velocity + substep_time * (acceleration / 2.0 + substep_time * jerk_rate / 6.0)
        )
        guess_vel = velocity + substep_time * (acceleration + substep_time * jerk_rate / 2.0)
        new_acc, new_jerk = evaluate(guess_pos, guess_vel)
        new_vel = (
            velocity
            + substep_time / 2.0 * (acceleration + new_acc)
            + substep_time * substep_time / 12.0 * (jerk_rate - new_jerk)
        )
        new_pos = (
            positions
            + substep_time / 2.0 * (velocity + new_vel)
            + substep_time * substep_time / 12.0 * (acceleration - new_acc)
        )
        positions, velocity, acceleration, jerk_rate = (new_pos, new_vel, new_acc, new_jerk)
    second_pull, second_push = kick(positions, body_pos)
    return (
        positions,
        velocity + half_step * second_pull,
        body_pos,
        body_vel + half_step * second_push,
    )


def solution(mesh):
    return jax.shard_map(
        local,
        mesh=mesh,
        in_specs=(
            P(None, "sub"),
            P(None, "sub"),
            P("sub"),
            P(None, ("grp", "sub")),
            P(None, ("grp", "sub")),
            P(("grp", "sub")),
            P(),
        ),
        out_specs=(
            P(None, "sub"),
            P(None, "sub"),
            P(None, ("grp", "sub")),
            P(None, ("grp", "sub")),
        ),
        check_vma=False,
    )
```

profile of v0, /device:TPU:0, one launch (start us, length us, event | category | flops | bytes accessed | tf_op | source)
XLA Modules:
  0.0 430.7 jit_solution(15473085354439461113)
XLA Ops:
  0.6 0.7 multiply_bitcast_fusion
  1.3 0.7 pad_maximum_fusion.10
  2.0 0.8 select_reduce_fusion
  2.8 27.8 %all_gather.33 = f32[4,1024]{1,0:T(4,128)S(1)} all-gather(f32[4,128]{1,0:T(4,128)S(1)} %pad_maximum_fusion.10), channel_id=1, replica_groups=mesh['grp'=4,'sub'=8] {'sub'}, dimensions={1}, use_global_device_ids=true | all-gather | bytes 18432 | tf_op jit(solution)/shard_map/all_gather | solution.py:81
  30.6 1.6 fusion.2
  32.8 0.8 fusion.3
  33.7 0.9 fusion
  35.0 1.2 fusion.1
  36.3 39.0 %psum.14 = f32[3,1024]{1,0:T(4,128)S(1)} all-reduce(f32[3,1024]{1,0:T(4,128)S(1)} %fusion.1), channel_id=1, replica_groups=mesh['grp'=4,'sub'=8] {'grp','sub'}, use_global_device_ids=true, to_apply=%region_3.4 | all-reduce | flops 3072 | bytes 24576 | tf_op jit(solution)/shard_map/psum | solution.py:84
  75.3 30.4 %all_gather.34 = f32[7,1024]{1,0:T(8,128)S(1)} all-gather(f32[7,128]{1,0:T(8,128)S(1)} %pad_maximum_fusion.8), channel_id=1, replica_groups=mesh['grp'=4,'sub'=8] {'sub'}, dimensions={1}, use_global_device_ids=true | all-gather | bytes 32256 | tf_op jit(solution)/shard_map/all_gather | solution.py:93
  106.3 0.7 fusion.27
  107.0 30.4 %all_gather.35 = f32[7,1024]{1,0:T(8,128)S(1)} all-gather(f32[7,128]{1,0:T(8,128)S(1)} %pad_maximum_fusion.7), channel_id=1, replica_groups=mesh['grp'=4,'sub'=8] {'sub'}, dimensions={1}, use_global_device_ids=true | all-gather | bytes 32256 | tf_op jit(solution)/shard_map/all_gather | solution.py:93
  138.0 0.7 fusion.11
  138.7 30.4 %all_gather.36 = f32[7,1024]{1,0:T(8,128)S(1)} all-gather(f32[7,128]{1,0:T(8,128)S(1)} %pad_maximum_fusion.6), channel_id=1, replica_groups=mesh['grp'=4,'sub'=8] {'sub'}, dimensions={1}, use_global_device_ids=true | all-gather | bytes 32256 | tf_op jit(solution)/shard_map/all_gather | solution.py:93
  169.7 0.7 fusion.13
  170.4 30.4 %all_gather.37 = f32[7,1024]{1,0:T(8,128)S(1)} all-gather(f32[7,128]{1,0:T(8,128)S(1)} %pad_maximum_fusion.5), channel_id=1, replica_groups=mesh['grp'=4,'sub'=8] {'sub'}, dimensions={1}, use_global_device_ids=true | all-gather | bytes 32256 | tf_op jit(solution)/shard_map/all_gather | solution.py:93
  201.4 0.7 fusion.15
  202.1 30.4 %all_gather.38 = f32[7,1024]{1,0:T(8,128)S(1)} all-gather(f32[7,128]{1,0:T(8,128)S(1)} %pad_maximum_fusion.4), channel_id=1, replica_groups=mesh['grp'=4,'sub'=8] {'sub'}, dimensions={1}, use_global_device_ids=true | all-gather | bytes 32256 | tf_op jit(solution)/shard_map/all_gather | solution.py:93
  233.0 0.7 fusion.17
  233.8 30.6 %all_gather.39 = f32[7,1024]{1,0:T(8,128)S(1)} all-gather(f32[7,128]{1,0:T(8,128)S(1)} %pad_maximum_fusion.3), channel_id=1, replica_groups=mesh['grp'=4,'sub'=8] {'sub'}, dimensions={1}, use_global_device_ids=true | all-gather | bytes 32256 | tf_op jit(solution)/shard_map/all_gather | solution.py:93
  264.9 0.7 fusion.19
  265.6 30.4 %all_gather.40 = f32[7,1024]{1,0:T(8,128)S(1)} all-gather(f32[7,128]{1,0:T(8,128)S(1)} %pad_maximum_fusion.2), channel_id=1, replica_groups=mesh['grp'=4,'sub'=8] {'sub'}, dimensions={1}, use_global_device_ids=true | all-gather | bytes 32256 | tf_op jit(solution)/shard_map/all_gather | solution.py:93
  296.6 0.7 fusion.21
  297.3 30.4 %all_gather.41 = f32[7,1024]{1,0:T(8,128)S(1)} all-gather(f32[7,128]{1,0:T(8,128)S(1)} %pad_maximum_fusion.1), channel_id=1, replica_groups=mesh['grp'=4,'sub'=8] {'sub'}, dimensions={1}, use_global_device_ids=true | all-gather | bytes 32256 | tf_op jit(solution)/shard_map/all_gather | solution.py:93
  328.3 0.7 fusion.23
  329.0 30.4 %all_gather.42 = f32[7,1024]{1,0:T(8,128)S(1)} all-gather(f32[7,128]{1,0:T(8,128)S(1)} %pad_maximum_fusion), channel_id=1, replica_groups=mesh['grp'=4,'sub'=8] {'sub'}, dimensions={1}, use_global_device_ids=true | all-gather | bytes 32256 | tf_op jit(solution)/shard_map/all_gather | solution.py:93
  360.0 0.7 fusion.25
  360.7 26.0 %all_gather.43 = f32[4,1024]{1,0:T(4,128)S(1)} all-gather(f32[4,128]{1,0:T(4,128)S(1)} %pad_maximum_fusion.9), channel_id=1, replica_groups=mesh['grp'=4,'sub'=8] {'sub'}, dimensions={1}, use_global_device_ids=true | all-gather | bytes 18432 | tf_op jit(solution)/shard_map/all_gather | solution.py:81
  387.7 0.8 fusion.7
  389.1 0.9 fusion.4
  390.5 1.2 fusion.5
  391.7 38.4 %psum.15 = f32[3,1024]{1,0:T(4,128)S(1)} all-reduce(f32[3,1024]{1,0:T(4,128)S(1)} %fusion.5), channel_id=1, replica_groups=mesh['grp'=4,'sub'=8] {'grp','sub'}, use_global_device_ids=true, to_apply=%region_44.45 | all-reduce | flops 3072 | bytes 24576 | tf_op jit(solution)/shard_map/psum | solution.py:84
  (82 shorter events, 8.8 us)
Async XLA Ops:
  32.1 0.7 copy-start
  32.8 0.8 copy-start.3
  33.7 356.8 %copy-start.1 = (f32[3,512]{1,0:T(4,128)}, f32[3,512]{1,0:T(4,128)S(1)}, u32[]{:S(2)}) copy-start(f32[3,512]{1,0:T(4,128)S(1)} %multiply_add_fusion.1) | copy-start | bytes 18436
  35.0 40.3 %copy-start.5 = (f32[3,128]{1,0:T(4,128)S(1)}, f32[3,128]{1,0:T(4,128)}, u32[]{:S(2)}) copy-start(f32[3,128]{1,0:T(4,128)} %param.8) | copy-start | bytes 4612
  35.0 40.3 %copy-start.2 = (f32[3,128]{1,0:T(4,128)S(1)}, f32[3,128]{1,0:T(4,128)}, u32[]{:S(2)}) copy-start(f32[3,128]{1,0:T(4,128)} %param.7) | copy-start | bytes 4612
  360.6 27.0 %copy-start.4 = (f32[3,128]{1,0:T(4,128)}, f32[3,128]{1,0:T(4,128)S(1)}, u32[]{:S(2)}) copy-start(f32[3,128]{1,0:T(4,128)S(1)} %multiply_add_fusion.4) | copy-start | bytes 4612
where the time goes:
time: 431 us
  blocking collectives  405 us (94%)
  other arithmetic  23.9 us (6%)
    all_gather x9, blocking collectives, evaluate(): source_piece = lax.all_gather(sources, 'sub', axis=1, tiled=True)  274 us
    psum x2, blocking collectives, kick(): summed = lax.psum(partial_value, ('grp', 'sub'))  77.5 us
    all_gather x2, blocking collectives, kick(): gathered = lax.all_gather(stacked, 'sub', axis=1, tiled=True)  53.8 us

commit v1 on v0

v1 whole, which is shorter than its diff:
```python
import functools

import jax
import jax.numpy as jnp
from jax import lax
from jax.experimental import pallas as pl
from jax.experimental.pallas import tpu as pltpu
from jax.sharding import PartitionSpec as P

SUBSTEPS = 8

step_time = 0.5
bridge_soft = 0.01
cluster_soft = 0.0025
f32 = jnp.float32
bf16 = jnp.bfloat16
vmem_limit = 48 * 1024 * 1024


def parts(x, count):
    terms = []
    for _ in range(count):
        term = x.astype(bf16).astype(f32)
        terms.append(term)
        x = x - term
    return terms


def rows(pieces, total):
    have = sum(piece.shape[0] for piece in pieces)
    if have < total:
        pieces = pieces + [jnp.zeros((total - have, pieces[0].shape[1]), f32)]
    return jnp.concatenate(pieces, axis=0)


def dot(a, b):
    return lax.dot_general(a, b, (((1,), (0,)), ((), ())), preferred_element_type=f32)


def dot_t(a, b):
    return lax.dot_general(a, b, (((1,), (1,)), ((), ())), preferred_element_type=f32)


def square(x):
    return jnp.sum(x * x, axis=0, keepdims=True)


def distance_from(pos, scale, soften):
    a = parts(-2.0 * scale * pos, 3)
    s = parts(scale, 3)
    e = parts(scale * (square(pos) + soften), 3)
    return rows(
        [a[0], a[0], a[0], a[1], a[1], a[2], s[0], s[0], s[0], s[1], s[1], s[2], *e], 32
    )


def distance_to(pos):
    p = parts(pos, 3)
    q = parts(square(pos), 3)
    one = jnp.ones_like(q[0])
    return rows(
        [p[0], p[1], p[2], p[0], p[1], p[0], q[0], q[1], q[2], q[0], q[1], q[0], one, one, one], 32
    )


def closing_from(pos, vel, scale):
    b = parts(-3.0 * scale * pos, 2)
    w = parts(-3.0 * scale * vel, 2)
    k = parts(3.0 * scale, 2)
    d = parts(3.0 * scale * jnp.sum(pos * vel, axis=0, keepdims=True), 2)
    return rows([b[0], b[0], b[1], w[0], w[0], w[1], k[0], k[0], k[1], *d], 32)


def closing_to(pos, vel):
    p = parts(pos, 2)
    v = parts(vel, 2)
    c = parts(jnp.sum(pos * vel, axis=0, keepdims=True), 2)
    one = jnp.ones_like(c[0])
    return rows([v[0], v[1], v[0], p[0], p[1], p[0], c[0], c[1], c[0], one, one], 32)


def split_rows(pos):
    return parts(pos, 3) + [jnp.ones_like(pos[:1])]


def moment(total, pos):
    return total[0:3] + total[3:6] + total[6:9] - pos * total[9:10]


def block_of(count, most):
    size = most
    while count % size:
        size //= 2
    return size


def evaluate(pos, vel, scale, from_ref, to_ref, sum_ref, out_ref):
    n = pos.shape[1]
    fill = jnp.concatenate(
        [distance_from(pos, scale, cluster_soft), closing_from(pos, vel, scale)], axis=0
    )
    from_ref[...] = fill.T.astype(bf16)
    to_ref[0:32, :] = distance_to(pos).astype(bf16)
    to_ref[32:64, :] = closing_to(pos, vel).astype(bf16)
    sum_ref[...] = jnp.concatenate(split_rows(pos) + parts(vel, 2), axis=0).astype(bf16)
    ti = block_of(n, 1024)
    tj = block_of(n, 256)

    def one_block(j, carry):
        lanes = pl.ds(j, tj)
        weight_sum = jnp.zeros((16, tj), f32)
        radial_sum = jnp.zeros((16, tj), f32)
        for i in range(0, n, ti):
            across = slice(i, i + ti)
            distance = dot(from_ref[across, 0:32], to_ref[0:32, lanes])
            closing = dot(from_ref[across, 32:64], to_ref[32:64, lanes])
            inverse = lax.rsqrt(distance)
            square_inverse = inverse * inverse
            weight = square_inverse * inverse
            radial = weight * square_inverse * closing
            high = weight.astype(bf16)
            low = (weight - high.astype(f32)).astype(bf16)
            radial_high = radial.astype(bf16)
            radial_low = (radial - radial_high.astype(f32)).astype(bf16)
            source = sum_ref[:, across]
            weight_sum += dot(source, high) + dot(source, low)
            radial_sum += dot(source, radial_high) + dot(source, radial_low)
        out_ref[0:16, lanes] = weight_sum
        out_ref[16:32, lanes] = radial_sum
        return carry

    if n // tj <= 4:
        for j in range(0, n, tj):
            one_block(j, 0)
    else:
        lax.fori_loop(0, n // tj, lambda k, c: one_block(pl.multiple_of(k * tj, tj), c), 0)
    total = out_ref[...]
    acceleration = moment(total, pos)
    jerk_rate = total[10:13] + total[13:16] - vel * total[9:10] - moment(total[16:32], pos)
    return acceleration, jerk_rate


def add_up(refs):
    values = [ref[...] for ref in refs]
    while len(values) > 1:
        values = [a + b for a, b in zip(values[::2], values[1::2])]
    return values[0]


def hermite_kernel(pull_count, stars_ref, *refs):
    pulls, (stars_out, pos_out, vel_out, from_ref, to_ref, sum_ref, out_ref) = (
        refs[:pull_count],
        refs[pull_count:],
    )
    own = pos_out.shape[1]
    pos = stars_ref[0:3, :]
    vel = stars_ref[3:6, :] + (step_time / 2.0) * add_up(pulls)
    scale = stars_ref[7:8, :]
    middle = jnp.mean(pos, axis=1, keepdims=True)
    drift = jnp.mean(vel, axis=1, keepdims=True)
    h = step_time / SUBSTEPS

    def rates(x, v):
        return evaluate(x, v, scale, from_ref, to_ref, sum_ref, out_ref)

    pos = pos - middle
    vel = vel - drift
    acc, jerk = rates(pos, vel)

    def substep(_, carry):
        pos, vel, acc, jerk = carry
        guess_pos = pos + h * (vel + h * (acc * 0.5 + (h / 6.0) * jerk))
        guess_vel = vel + h * (acc + (h / 2.0) * jerk)
        new_acc, new_jerk = rates(guess_pos, guess_vel)
        new_vel = vel + (h / 2.0) * (acc + new_acc) + (h * h / 12.0) * (jerk - new_jerk)
        new_pos = pos + (h / 2.0) * (vel + new_vel) + (h * h / 12.0) * (acc - new_acc)
        return new_pos, new_vel, new_acc, new_jerk

    pos, vel, _, _ = lax.fori_loop(0, SUBSTEPS, substep, (pos, vel, acc, jerk))
    pos = pos + (middle + step_time * drift)
    vel = vel + drift
    stars_out[...] = jnp.concatenate([pos, vel, stars_ref[6:8, :]], axis=0)
    pos_out[...] = pos[:, :own]
    vel_out[...] = vel[:, :own]


def hermite(stars, pulls, own):
    n = stars.shape[1]
    pairs = n * n * (SUBSTEPS + 1)
    return pl.pallas_call(
        functools.partial(hermite_kernel, len(pulls)),
        out_shape=[
            jax.ShapeDtypeStruct(stars.shape, f32),
            jax.ShapeDtypeStruct((3, own), f32),
            jax.ShapeDtypeStruct((3, own), f32),
        ],
        scratch_shapes=[
            pltpu.VMEM((n, 64), bf16),
            pltpu.VMEM((64, n), bf16),
            pltpu.VMEM((16, n), bf16),
            pltpu.VMEM((32, n), f32),
        ],
        compiler_params=pltpu.CompilerParams(vmem_limit_bytes=vmem_limit),
        cost_estimate=pl.CostEstimate(flops=80 * pairs, bytes_accessed=0, transcendentals=pairs),
    )(stars, *pulls)


def center_of(stars, bodies):
    return 0.5 * (
        jnp.mean(stars, axis=1, keepdims=True) + jnp.mean(bodies, axis=1, keepdims=True)
    )


def weights(from_rows, to_columns):
    inverse = lax.rsqrt(dot(from_rows, to_columns))
    return inverse * inverse * inverse


def dot_high(sums, weight):
    return dot(sums, weight.astype(bf16))


def dot_both(sums, weight):
    high = weight.astype(bf16)
    return dot(sums, high) + dot(sums, (weight - high.astype(f32)).astype(bf16))


def kick_kernel(star_own, piece_count, *refs):
    pieces, (stars_out, bodies_out, pull_out, pos_out, vel_out, from_ref, sum_ref, pull_ref) = (
        refs[:piece_count],
        refs[piece_count:],
    )
    body_own = pos_out.shape[1]
    slot = 0
    for piece in pieces:
        for k in range(piece.shape[0]):
            stars_out[:, slot * star_own : (slot + 1) * star_own] = piece[k, :, :star_own]
            bodies_out[:, slot * body_own : (slot + 1) * body_own] = piece[k, :, star_own:]
            slot += 1
    n, count = stars_out.shape[1], bodies_out.shape[1]
    middle = center_of(stars_out[0:3, :], bodies_out[0:3, :])
    star_pos = stars_out[0:3, :] - middle
    scale = stars_out[7:8, :]
    from_ref[...] = distance_from(star_pos, scale, bridge_soft).T.astype(bf16)
    sum_ref[...] = rows(split_rows(star_pos), 16).astype(bf16)
    pull_ref[...] = jnp.zeros_like(pull_ref)
    ti = block_of(n, 1024)
    tj = block_of(body_own, 256)

    def one_block(j, multiply):
        lanes = pl.ds(j, tj)
        body_pos = bodies_out[0:3, lanes] - middle
        body_vel = bodies_out[3:6, lanes]
        mass = bodies_out[6:7, lanes]
        to = distance_to(body_pos).astype(bf16)
        moments = rows(parts(mass * body_pos, 3) + parts(mass, 3), 16).astype(bf16)
        push = jnp.zeros((16, tj), f32)
        for i in range(0, n, ti):
            weight = weights(from_ref[i : i + ti, :], to)
            push += multiply(sum_ref[:, i : i + ti], weight)
            pull_ref[:, i : i + ti] += dot_t(moments, weight.astype(bf16))
        body_vel = body_vel + (step_time / 2.0) * moment(push, body_pos)
        body_pos = body_pos + middle + step_time * body_vel
        bodies_out[0:3, lanes] = body_pos
        bodies_out[3:6, lanes] = body_vel

    for j in range(0, body_own, tj):
        one_block(j, dot_both)

    def other_block(k, carry):
        one_block(pl.multiple_of(k * tj, tj), dot_high)
        return carry

    lax.fori_loop(body_own // tj, count // tj, other_block, 0)
    pull = pull_ref[...]
    mass_sum = pull[9:10] + pull[10:11] + pull[11:12]
    pull_out[...] = (pull[0:3] + pull[3:6] + pull[6:9] - star_pos * mass_sum) / stars_out[6:7, :]
    pos_out[...] = bodies_out[0:3, :body_own]
    vel_out[...] = bodies_out[3:6, :body_own]


def first_kick(pieces, star_own):
    blocks = sum(piece.shape[0] for piece in pieces)
    body_own = pieces[0].shape[2] - star_own
    n, count = blocks * star_own, blocks * body_own
    pairs = n * count
    return pl.pallas_call(
        functools.partial(kick_kernel, star_own, len(pieces)),
        out_shape=[
            jax.ShapeDtypeStruct((8, n), f32),
            jax.ShapeDtypeStruct((8, count), f32),
            jax.ShapeDtypeStruct((3, n), f32),
            jax.ShapeDtypeStruct((3, body_own), f32),
            jax.ShapeDtypeStruct((3, body_own), f32),
        ],
        scratch_shapes=[
            pltpu.VMEM((n, 32), bf16),
            pltpu.VMEM((16, n), bf16),
            pltpu.VMEM((16, n), f32),
        ],
        compiler_params=pltpu.CompilerParams(vmem_limit_bytes=vmem_limit),
        cost_estimate=pl.CostEstimate(flops=40 * pairs, bytes_accessed=0, transcendentals=pairs),
    )(*pieces)


def pull_kernel(stars_ref, bodies_ref, pull_out):
    own, count = pull_out.shape[1], bodies_ref.shape[1]
    middle = center_of(stars_ref[0:3, :], bodies_ref[0:3, :])
    star_pos = stars_ref[0:3, :own] - middle
    source = distance_from(star_pos, stars_ref[7:8, :own], bridge_soft).T.astype(bf16)
    tj = block_of(count, 1024)

    def one_block(k, pull):
        lanes = pl.ds(pl.multiple_of(k * tj, tj), tj)
        body_pos = bodies_ref[0:3, lanes] - middle
        mass = bodies_ref[6:7, lanes]
        to = distance_to(body_pos).astype(bf16)
        moments = rows(parts(mass * body_pos, 3) + parts(mass, 3), 16).astype(bf16)
        return pull + dot_t(moments, weights(source, to).astype(bf16))

    pull = lax.fori_loop(0, count // tj, one_block, jnp.zeros((16, own), f32))
    mass_sum = pull[9:10] + pull[10:11] + pull[11:12]
    pull_out[...] = (pull[0:3] + pull[3:6] + pull[6:9] - star_pos * mass_sum) / stars_ref[
        6:7, :own
    ]


def second_pull(stars, bodies, own):
    pairs = own * bodies.shape[1]
    return pl.pallas_call(
        pull_kernel,
        out_shape=jax.ShapeDtypeStruct((3, own), f32),
        compiler_params=pltpu.CompilerParams(vmem_limit_bytes=vmem_limit),
        cost_estimate=pl.CostEstimate(flops=40 * pairs, bytes_accessed=0, transcendentals=pairs),
    )(stars, bodies)


def push_kernel(stars_ref, pos_ref, vel_ref, vel_out):
    n = stars_ref.shape[1]
    middle = center_of(stars_ref[0:3, :], pos_ref[...])
    star_pos = stars_ref[0:3, :] - middle
    body_pos = pos_ref[...] - middle
    source = distance_from(star_pos, stars_ref[7:8, :], bridge_soft).T.astype(bf16)
    to = distance_to(body_pos).astype(bf16)
    sums = rows(split_rows(star_pos), 16).astype(bf16)
    ti = block_of(n, 1024)
    push = jnp.zeros((16, body_pos.shape[1]), f32)
    for i in range(0, n, ti):
        push += dot_both(sums[:, i : i + ti], weights(source[i : i + ti], to))
    vel_out[...] = vel_ref[...] + (step_time / 2.0) * moment(push, body_pos)


def second_push(stars, body_pos, body_vel):
    pairs = stars.shape[1] * body_pos.shape[1]
    return pl.pallas_call(
        push_kernel,
        out_shape=jax.ShapeDtypeStruct(body_vel.shape, f32),
        compiler_params=pltpu.CompilerParams(vmem_limit_bytes=vmem_limit),
        cost_estimate=pl.CostEstimate(flops=40 * pairs, bytes_accessed=0, transcendentals=pairs),
    )(stars, body_pos, body_vel)


def swap(x, axis, bits):
    count = lax.axis_size(axis)
    return lax.ppermute(x, axis, [(i, i ^ bits) for i in range(count)])


def radices(count):
    steps, bit = [], 1
    if count.bit_length() % 2 == 0:
        steps.append((1,))
        bit = 2
    while bit < count:
        steps.append((bit, 2 * bit, 3 * bit))
        bit *= 4
    return steps


def gather_pieces(x, axis):
    pieces = [x[None]]
    for step in radices(lax.axis_size(axis)):
        if len(pieces) > 1:
            pieces = [jnp.concatenate(pieces, axis=0)]
        pieces = pieces + [swap(pieces[0], axis, bits) for bits in step]
    return pieces


def sum_pieces(x, axis):
    pieces = [x]
    for step in radices(lax.axis_size(axis)):
        while len(pieces) > 1:
            pieces = [a + b for a, b in zip(pieces[::2], pieces[1::2])]
        pieces = pieces + [swap(pieces[0], axis, bits) for bits in step]
    return pieces


def local(
    cluster_pos, cluster_vel, cluster_mass, galaxy_pos, galaxy_vel, galaxy_kind, species_mass
):
    own = cluster_pos.shape[1]
    total_stars = own * lax.axis_size("sub")
    total_bodies = galaxy_pos.shape[1] * lax.axis_size("sub") * lax.axis_size("grp")
    star_mass = cluster_mass / total_stars
    species = jnp.arange(species_mass.shape[0], dtype=jnp.int32)
    body_mass = (
        jnp.sum(
            jnp.where(galaxy_kind[None, :] == species[:, None], species_mass[:, None], 0.0), axis=0
        )
        / total_bodies
    )
    scale = jnp.exp(jnp.log(star_mass) * (-2.0 / 3.0))
    stars = jnp.concatenate([cluster_pos, cluster_vel, star_mass[None], scale[None]], axis=0)
    bodies = jnp.concatenate(
        [galaxy_pos, galaxy_vel, body_mass[None], jnp.zeros_like(body_mass)[None]], axis=0
    )
    pieces = gather_pieces(jnp.concatenate([stars, bodies], axis=1), "sub")
    all_stars, all_bodies, pull, body_pos, body_vel = first_kick(pieces, own)
    end_stars, end_pos, end_vel = hermite(all_stars, sum_pieces(pull, "grp"), own)
    pull = second_pull(end_stars, all_bodies, own)
    pulls = sum_pieces(pull, "grp")
    body_vel = second_push(end_stars, body_pos, body_vel)
    while len(pulls) > 1:
        pulls = [a + b for a, b in zip(pulls[::2], pulls[1::2])]
    return end_pos, end_vel + (step_time / 2.0) * pulls[0], body_pos, body_vel


def solution(mesh):
    return jax.shard_map(
        local,
        mesh=mesh,
        in_specs=(
            P(None, "sub"),
            P(None, "sub"),
            P("sub"),
            P(None, ("grp", "sub")),
            P(None, ("grp", "sub")),
            P(("grp", "sub")),
            P(),
        ),
        out_specs=(
            P(None, "sub"),
            P(None, "sub"),
            P(None, ("grp", "sub")),
            P(None, ("grp", "sub")),
        ),
        check_vma=False,
    )
```

time: 431 us -> 68.1 us (0.16)
  blocking collectives: 405 us -> 0 us
  Pallas kernels: 0 us -> 44.2 us
  other arithmetic: 23.9 us -> 2.76 us
  starting transfers between devices: 0 us -> 11.8 us
  waiting for transfers between devices: 0 us -> 8.41 us
    all_gather x11 -> x0, blocking collectives: 328 us -> none  [the longest x9 274 us: evaluate(): source_piece = lax.all_gather(sources, 'sub', axis=1, tiled=True)]
    psum x2 -> x0, blocking collectives: 77.5 us -> none  [kick(): summed = lax.psum(partial_value, ('grp', 'sub'))]
    pallas_call x0 -> x4, Pallas kernels: none -> 44.2 us  [the longest x1 28.6 us: hermite(): pl.pallas_call(functools.partial(hermite_kernel, len(pulls)), out_shape=[...]
    reduce_sum x26 -> x0, other arithmetic: 17.6 us -> none  [the longest x8 5.29 us: rates_one_tile(): jnp.sum((closing - radial[None] * separation) * weight[None], axis=2)]
    ppermute x0 -> x10, starting transfers between devices: none -> 11.8 us  [swap(): return lax.ppermute(x, axis, [(i, i ^ bits) for i in range(count)])]
    ppermute x0 -> x10, waiting for transfers between devices: none -> 8.41 us  [swap(): return lax.ppermute(x, axis, [(i, i ^ bits) for i in range(count)])]
  transfers between devices with their start and end apart: 0 -> 10, of which waited for: 0 -> 6; matrix products, arithmetic and copies ran while one was open for 0% -> 0% of each run, Pallas kernels for 0% -> 2%
where the time goes in v1:
time: 68.1 us; the launch traced here: 67.9 us
  Pallas kernels  44.2 us (65%)
  starting transfers between devices  11.8 us (17%)
  waiting for transfers between devices  8.41 us (12%)
  other arithmetic  2.76 us (4%)
  between operations  0.71 us (1%)
    pallas_call x1, Pallas kernels, hermite(): pl.pallas_call(functools.partial(hermite_kernel, len(pulls)), out_shape=[...  28.6 us
    pallas_call x1, Pallas kernels, first_kick(): pl.pallas_call(functools.partial(kick_kernel, star_own, len(pieces)), out...  12.3 us
    ppermute x10, starting transfers between devices, swap(): return lax.ppermute(x, axis, [(i, i ^ bits) for i in range(count)])  11.8 us
    ppermute x10, waiting for transfers between devices, swap(): return lax.ppermute(x, axis, [(i, i ^ bits) for i in range(count)])  8.41 us
    pallas_call x1, Pallas kernels, second_pull(): pl.pallas_call(pull_kernel, out_shape=jax.ShapeDtypeStruct((3, own), f32)...  1.68 us
    pallas_call x1, Pallas kernels, second_push(): pl.pallas_call(push_kernel, out_shape=jax.ShapeDtypeStruct(body_vel.shape...  1.67 us
  transfers between devices with their start and end apart: 10, of which 6 were waited for; matrix products, arithmetic and copies ran while one was open for 0% of the time, Pallas kernels for 2%

profile of v1, /device:TPU:0, one launch (start us, length us, event | category | flops | bytes accessed | tf_op | source)
XLA Modules:
  0.0 67.9 jit_solution(8152813725920349427)
XLA Ops:
  0.6 0.0 copy-start.4
  0.6 0.0 copy-start.3
  0.7 0.7 multiply_bitcast_fusion
  1.3 0.0 copy-done.4
  1.3 0.0 copy-start.2
  1.3 0.8 %select_reduce_fusion = f32[512]{0:T(512)S(1)} fusion(f32[4]{0:T(128)S(1)} %copy-done.4, s32[512]{0:T(512)} %param.12), kind=kLoop, calls=%fused_computation.2 | loop fusion | flops 5632 | bytes 4112 | tf_op jit(solution)/shard_map/reduce_sum | solution.py:406
  2.2 0.7 %maximum_bitcast_fusion = f32[1,8,640]{2,1,0:T(8,128)S(1)} fusion(f32[1,512]{1,0:T(1,128)S(1)} %broadcast_in_dim_broadcast_in_dim.3, f32[1,512]{1,0:T(1,128)S(1)} %bitcast.7, f32[3,512]{1,0:T(4,128)S(1)} %copy-done.1, f32[3,512]{1,0:T(4,128)S(1)} %copy-done.2, f32[1,128]{1,0:T(1,128)S(1)} %get-tuple-element.21, f32[1,128]{1,0:T(1,128)S(1)} %get-tuple-element.20, ...), kind=kLoop, calls=%fused_computation.1 | loop fusion | flops 35840 | bytes 40960 | tf_op jit(solution)/shard_map/broadcast_in_dim | solution.py:380
  2.9 3.0 %collective-permute-start = (f32[1,8,640]{2,1,0:T(8,128)S(1)}, f32[1,8,640]{2,1,0:T(8,128)S(1)}, u32[]{:S(2)}, u32[]{:S(2)}) collective-permute-start(f32[1,8,640]{2,1,0:T(8,128)S(1)} %maximum_bitcast_fusion), channel_id=1, source_target_pairs={{0,1},{1,0},{2,3},{3,2},{4,5},{5,4},{6,7},{7,6},{8,9},{9,8},{10,11... | collective-permute-start | bytes 61448 | tf_op jit(solution)/shard_map/ppermute | solution.py:365
  5.9 1.8 %collective-permute-done = f32[1,8,640]{2,1,0:T(8,128)S(1)} collective-permute-done((f32[1,8,640]{2,1,0:T(8,128)S(1)}, f32[1,8,640]{2,1,0:T(8,128)S(1)}, u32[]{:S(2)}, u32[]{:S(2)}) %collective-permute-start) | collective-permute-done | bytes 20512 | tf_op jit(solution)/shard_map/ppermute | solution.py:365
  7.7 4.1 %collective-permute-start.3 = (f32[2,8,640]{2,1,0:T(8,128)S(1)}, f32[2,8,640]{2,1,0:T(8,128)S(1)}, u32[]{:S(2)}, u32[]{:S(2)}) collective-permute-start(f32[2,8,640]{2,1,0:T(8,128)S(1)} %pad_maximum_fusion.refs_0_), channel_id=1, source_target_pairs={{0,6},{1,7},{2,4},{3,5},{4,2},{5,3},{6,0},{7,1},{8,14},{9,15},{10,... | collective-permute-start | bytes 122888 | tf_op jit(solution)/shard_map/ppermute | solution.py:365
  11.8 0.0 collective-permute-start.2
  11.8 0.6 collective-permute-start.1
  12.4 1.4 %collective-permute-done.3.refs_3_ = f32[2,8,640]{2,1,0:T(8,128)S(1)} collective-permute-done((f32[2,8,640]{2,1,0:T(8,128)S(1)}, f32[2,8,640]{2,1,0:T(8,128)S(1)}, u32[]{:S(2)}, u32[]{:S(2)}) %collective-permute-start.3) | collective-permute-done | bytes 40992 | tf_op jit(solution)/shard_map/ppermute | solution.py:365
  13.8 2.9 %collective-permute-done.2.refs_2_ = f32[2,8,640]{2,1,0:T(8,128)S(1)} collective-permute-done((f32[2,8,640]{2,1,0:T(8,128)S(1)}, f32[2,8,640]{2,1,0:T(8,128)S(1)}, u32[]{:S(2)}, u32[]{:S(2)}) %collective-permute-start.2) | collective-permute-done | bytes 40992 | tf_op jit(solution)/shard_map/ppermute | solution.py:365
  16.7 0.0 collective-permute-done.1.refs_1_
  16.7 12.3 %shard_map.102 = (f32[8,1024]{1,0:T(8,128)S(1)}, f32[8,4096]{1,0:T(8,128)S(1)}, f32[3,1024]{1,0:T(4,128)S(1)}, f32[3,512]{1,0:T(4,128)}, f32[3,512]{1,0:T(4,128)S(1)}) custom-call(f32[2,8,640]{2,1,0:T(8,128)S(1)} %pad_maximum_fusion.refs_0_, f32[2,8,640]{2,1,0:T(8,128)S(1)} %collective-permute-done.1.refs_1_, ...), custom_call_target="tpu_custom_call" | custom-call | flops 167772160 | tf_op jit(solution)/shard_map/pallas_call | solution.py:287
  29.0 0.0 collective-permute-start.6
  29.0 1.5 %collective-permute-start.5 = (f32[3,1024]{1,0:T(4,128)S(1)}, f32[3,1024]{1,0:T(4,128)S(1)}, u32[]{:S(2)}, u32[]{:S(2)}) collective-permute-start(f32[3,1024]{1,0:T(4,128)S(1)} %get-tuple-element.13.refs_0_), channel_id=1, source_target_pairs={{0,16},{8,24},{16,0},{24,8},{1,17},{9,25},{17,1},{25,9},{2,18},{10... | collective-permute-start | bytes 36872 | tf_op jit(solution)/shard_map/ppermute | solution.py:365
  30.6 0.3 collective-permute-start.4
  30.9 1.4 %collective-permute-done.6.refs_3_ = f32[3,1024]{1,0:T(4,128)S(1)} collective-permute-done((f32[3,1024]{1,0:T(4,128)S(1)}, f32[3,1024]{1,0:T(4,128)S(1)}, u32[]{:S(2)}, u32[]{:S(2)}) %collective-permute-start.6) | collective-permute-done | bytes 12320 | tf_op jit(solution)/shard_map/ppermute | solution.py:365
  32.3 0.5 collective-permute-done.5.refs_2_
  32.8 0.0 collective-permute-done.4.refs_1_
  32.8 28.6 %shard_map.103 = (f32[8,1024]{1,0:T(8,128)S(1)}, f32[3,128]{1,0:T(4,128)}, f32[3,128]{1,0:T(4,128)S(1)}) custom-call(f32[8,1024]{1,0:T(8,128)S(1)} %get-tuple-element.12.stars_ref, f32[3,1024]{1,0:T(4,128)S(1)} %get-tuple-element.13.refs_0_, f32[3,1024]{1,0:T(4,128)S(1)} %collective-permute-done.4.refs_1_, f32[3,1024]{1,0:T(4,128)S(1)} %collective-permute-done.5.refs_2_, ...), custom_call_target="tpu_custom_call" | custom-call | flops 754974720 | tf_op jit(solution)/shard_map/pallas_call | solution.py:190
  61.4 1.7 %shard_map.104 = f32[3,128]{1,0:T(4,128)S(1)} custom-call(f32[8,1024]{1,0:T(8,128)S(1)} %get-tuple-element.16.stars_ref, f32[8,4096]{1,0:T(8,128)S(1)} %get-tuple-element.17.bodies_ref), custom_call_target="tpu_custom_call" | custom-call | flops 20971520 | tf_op jit(solution)/shard_map/pallas_call | solution.py:330
  63.0 0.7 %collective-permute-start.9 = (f32[3,128]{1,0:T(4,128)S(1)}, f32[3,128]{1,0:T(4,128)S(1)}, u32[]{:S(2)}, u32[]{:S(2)}) collective-permute-start(f32[3,128]{1,0:T(4,128)S(1)} %shard_map.104), channel_id=1, source_target_pairs={{0,24},{8,16},{16,8},{24,0},{1,25},{9,17},{17,9},{25,1},{2,26},{10... | collective-permute-start | bytes 4616 | tf_op jit(solution)/shard_map/ppermute | solution.py:365
  63.7 1.5 %collective-permute-start.8 = (f32[3,128]{1,0:T(4,128)S(1)}, f32[3,128]{1,0:T(4,128)S(1)}, u32[]{:S(2)}, u32[]{:S(2)}) collective-permute-start(f32[3,128]{1,0:T(4,128)S(1)} %shard_map.104), channel_id=1, source_target_pairs={{0,16},{8,24},{16,0},{24,8},{1,17},{9,25},{17,1},{25,9},{2,18},{10... | collective-permute-start | bytes 4616 | tf_op jit(solution)/shard_map/ppermute | solution.py:365
  65.2 0.0 collective-permute-start.7
  65.2 1.7 %shard_map.105 = f32[3,512]{1,0:T(4,128)} custom-call(f32[8,1024]{1,0:T(8,128)S(1)} %get-tuple-element.16.stars_ref, f32[3,512]{1,0:T(4,128)S(1)} %copy-done, f32[3,512]{1,0:T(4,128)S(1)} %get-tuple-element.19.vel_ref), custom_call_target="tpu_custom_call" | custom-call | flops 20971520 | tf_op jit(solution)/shard_map/pallas_call | solution.py:355
  66.9 0.0 collective-permute-done.9
  66.9 0.5 collective-permute-done.8
  67.3 0.0 collective-permute-done.7
  67.3 0.6 multiply_add_fusion
  (9 shorter events, 0.0 us)
Async XLA Ops:
  0.6 0.7 %copy-start.4 = (f32[4]{0:T(128)S(1)}, f32[4]{0:T(128)}, u32[]{:S(2)}) copy-start(f32[4]{0:T(128)} %param.13) | copy-start | bytes 52
  0.6 1.5 %copy-start.3 = (f32[3,128]{1,0:T(4,128)S(1)}, f32[3,128]{1,0:T(4,128)}, u32[]{:S(2)}) copy-start(f32[3,128]{1,0:T(4,128)} %param.8) | copy-start | bytes 4612
  1.3 0.8 %copy-start.1 = (f32[3,512]{1,0:T(4,128)S(1)}, f32[3,512]{1,0:T(4,128)}, u32[]{:S(2)}) copy-start(f32[3,512]{1,0:T(4,128)} %param.11) | copy-start | bytes 18436
  1.3 0.8 %copy-start.2 = (f32[3,512]{1,0:T(4,128)S(1)}, f32[3,512]{1,0:T(4,128)}, u32[]{:S(2)}) copy-start(f32[3,512]{1,0:T(4,128)} %param.10) | copy-start | bytes 18436
  2.9 4.8 %collective-permute-start = (f32[1,8,640]{2,1,0:T(8,128)S(1)}, f32[1,8,640]{2,1,0:T(8,128)S(1)}, u32[]{:S(2)}, u32[]{:S(2)}) collective-permute-start(f32[1,8,640]{2,1,0:T(8,128)S(1)} %maximum_bitcast_fusion), channel_id=1, source_target_pairs={{0,1},{1,0},{2,3},{3,2},{4,5},{5,4},{6,7},{7,6},{8,9},{9,8},{10,11... | collective-permute-start | bytes 61448 | tf_op jit(solution)/shard_map/ppermute | solution.py:365
  7.7 6.1 %collective-permute-start.3 = (f32[2,8,640]{2,1,0:T(8,128)S(1)}, f32[2,8,640]{2,1,0:T(8,128)S(1)}, u32[]{:S(2)}, u32[]{:S(2)}) collective-permute-start(f32[2,8,640]{2,1,0:T(8,128)S(1)} %pad_maximum_fusion.refs_0_), channel_id=1, source_target_pairs={{0,6},{1,7},{2,4},{3,5},{4,2},{5,3},{6,0},{7,1},{8,14},{9,15},{10,... | collective-permute-start | bytes 122888 | tf_op jit(solution)/shard_map/ppermute | solution.py:365
  11.8 4.9 %collective-permute-start.2 = (f32[2,8,640]{2,1,0:T(8,128)S(1)}, f32[2,8,640]{2,1,0:T(8,128)S(1)}, u32[]{:S(2)}, u32[]{:S(2)}) collective-permute-start(f32[2,8,640]{2,1,0:T(8,128)S(1)} %pad_maximum_fusion.refs_0_), channel_id=1, source_target_pairs={{0,4},{1,5},{2,6},{3,7},{4,0},{5,1},{6,2},{7,3},{8,12},{9,13},{10,... | collective-permute-start | bytes 122888 | tf_op jit(solution)/shard_map/ppermute | solution.py:365
  11.8 4.9 %collective-permute-start.1 = (f32[2,8,640]{2,1,0:T(8,128)S(1)}, f32[2,8,640]{2,1,0:T(8,128)S(1)}, u32[]{:S(2)}, u32[]{:S(2)}) collective-permute-start(f32[2,8,640]{2,1,0:T(8,128)S(1)} %pad_maximum_fusion.refs_0_), channel_id=1, source_target_pairs={{0,2},{1,3},{2,0},{3,1},{4,6},{5,7},{6,4},{7,5},{8,10},{9,11},{10,... | collective-permute-start | bytes 122888 | tf_op jit(solution)/shard_map/ppermute | solution.py:365
  29.0 3.3 %collective-permute-start.6 = (f32[3,1024]{1,0:T(4,128)S(1)}, f32[3,1024]{1,0:T(4,128)S(1)}, u32[]{:S(2)}, u32[]{:S(2)}) collective-permute-start(f32[3,1024]{1,0:T(4,128)S(1)} %get-tuple-element.13.refs_0_), channel_id=1, source_target_pairs={{0,24},{8,16},{16,8},{24,0},{1,25},{9,17},{17,9},{25,1},{2,26},{10... | collective-permute-start | bytes 36872 | tf_op jit(solution)/shard_map/ppermute | solution.py:365
  29.0 3.8 %collective-permute-start.5 = (f32[3,1024]{1,0:T(4,128)S(1)}, f32[3,1024]{1,0:T(4,128)S(1)}, u32[]{:S(2)}, u32[]{:S(2)}) collective-permute-start(f32[3,1024]{1,0:T(4,128)S(1)} %get-tuple-element.13.refs_0_), channel_id=1, source_target_pairs={{0,16},{8,24},{16,0},{24,8},{1,17},{9,25},{17,1},{25,9},{2,18},{10... | collective-permute-start | bytes 36872 | tf_op jit(solution)/shard_map/ppermute | solution.py:365
  30.6 2.2 %collective-permute-start.4 = (f32[3,1024]{1,0:T(4,128)S(1)}, f32[3,1024]{1,0:T(4,128)S(1)}, u32[]{:S(2)}, u32[]{:S(2)}) collective-permute-start(f32[3,1024]{1,0:T(4,128)S(1)} %get-tuple-element.13.refs_0_), channel_id=1, source_target_pairs={{0,8},{8,0},{16,24},{24,16},{1,9},{9,1},{17,25},{25,17},{2,10},{10... | collective-permute-start | bytes 36872 | tf_op jit(solution)/shard_map/ppermute | solution.py:365
  61.4 3.8 %copy-start = (f32[3,512]{1,0:T(4,128)S(1)}, f32[3,512]{1,0:T(4,128)}, u32[]{:S(2)}) copy-start(f32[3,512]{1,0:T(4,128)} %get-tuple-element.10.pos_ref) | copy-start | bytes 18436
  63.0 3.8 %collective-permute-start.9 = (f32[3,128]{1,0:T(4,128)S(1)}, f32[3,128]{1,0:T(4,128)S(1)}, u32[]{:S(2)}, u32[]{:S(2)}) collective-permute-start(f32[3,128]{1,0:T(4,128)S(1)} %shard_map.104), channel_id=1, source_target_pairs={{0,24},{8,16},{16,8},{24,0},{1,25},{9,17},{17,9},{25,1},{2,26},{10... | collective-permute-start | bytes 4616 | tf_op jit(solution)/shard_map/ppermute | solution.py:365
  63.7 3.6 %collective-permute-start.8 = (f32[3,128]{1,0:T(4,128)S(1)}, f32[3,128]{1,0:T(4,128)S(1)}, u32[]{:S(2)}, u32[]{:S(2)}) collective-permute-start(f32[3,128]{1,0:T(4,128)S(1)} %shard_map.104), channel_id=1, source_target_pairs={{0,16},{8,24},{16,0},{24,8},{1,17},{9,25},{17,1},{25,9},{2,18},{10... | collective-permute-start | bytes 4616 | tf_op jit(solution)/shard_map/ppermute | solution.py:365
  65.2 2.1 %collective-permute-start.7 = (f32[3,128]{1,0:T(4,128)S(1)}, f32[3,128]{1,0:T(4,128)S(1)}, u32[]{:S(2)}, u32[]{:S(2)}) collective-permute-start(f32[3,128]{1,0:T(4,128)S(1)} %shard_map.104), channel_id=1, source_target_pairs={{0,8},{8,0},{16,24},{24,16},{1,9},{9,1},{17,25},{25,17},{2,10},{10... | collective-permute-start | bytes 4616 | tf_op jit(solution)/shard_map/ppermute | solution.py:365

commit v2 on v0

v2 whole, which is shorter than its diff:
```python
import functools

import jax
import jax.numpy as jnp
import numpy as np
from jax import lax
from jax.experimental import pallas as pl
from jax.experimental.pallas import tpu as pltpu
from jax.sharding import PartitionSpec as P

SUBSTEPS = 8

step_time = 0.5
bridge_soft = 0.01
cluster_soft = 0.0025
f32 = jnp.float32
bf16 = jnp.bfloat16
vmem_limit = 48 * 1024 * 1024


def parts(x, count):
    terms = []
    for _ in range(count):
        term = x.astype(bf16).astype(f32)
        terms.append(term)
        x = x - term
    return terms


def dot(a, b):
    return lax.dot_general(a, b, (((1,), (0,)), ((), ())), preferred_element_type=f32)


def dot_t(a, b):
    return lax.dot_general(a, b, (((1,), (1,)), ((), ())), preferred_element_type=f32)


def split(x):
    high = x.astype(bf16)
    return high, (x - high.astype(f32)).astype(bf16)


def block_of(count, most):
    size = most
    while count % size:
        size //= 2
    return size


def row_of(x):
    return lax.broadcasted_iota(jnp.int32, x.shape, 0)


def rot(x):
    return pltpu.roll(x, 4, 0)


def block(row, a, sa, b, sb):
    return jnp.where(row < 3, a, jnp.where(row == 3, sa, jnp.where(row < 7, b, sb)))


def constant_parts(value):
    terms = []
    for _ in range(3):
        term = float(np.asarray(value, bf16))
        terms.append(term)
        value -= term
    return terms


def fill(row, block, third, seventh):
    return jnp.where(row == 3, third, jnp.where(row == 7, seventh, block))


def grid_of(y):
    x = jnp.where(row_of(y) < 3, y, 0.0)
    grid = jnp.floor(x * 8.0 + 0.5) * 0.125
    rest = x - grid
    square = jnp.sum(grid * grid, axis=0, keepdims=True)
    return grid, rest, square, jnp.sum(rest * (grid + x), axis=0, keepdims=True)


def distance_rows(grid, rest, q, p, soften):
    row = row_of(grid)
    e = parts(rest, 3)
    f = [-2.0 * term for term in e]
    soft = constant_parts(soften)
    twice = -2.0 * grid
    rot_grid, rot_twice = rot(grid), rot(twice)
    rot_e, rot_f = rot(e[1]), rot(f[0])
    targets = [
        block(row, grid, q[0], jnp.where(row == 4, q[1], 1.0), 1.0),
        block(row, e[0], p[0], rot_e, p[1]),
        block(row, e[2], p[2], rot_grid, 1.0),
        block(row, grid, 1.0, rot_grid, 1.0),
        block(row, e[0], 1.0, rot_e, 1.0),
        e[0],
    ]
    last = jnp.where(row == 4, 1.0, jnp.where(row == 5, q[0], q[1]))
    sources = [
        block(row, twice, 1.0, last, soft[0]),
        block(row, twice, 1.0, rot_twice, 1.0),
        block(row, twice, 1.0, rot_f, p[0]),
        block(row, f[1], p[1], rot(f[2]), p[2]),
        block(row, f[0], soft[1], rot_f, soft[2]),
        f[1],
    ]
    return jnp.concatenate(sources, axis=0), jnp.concatenate(targets, axis=0)


def distance_blocks(y, soften):
    grid, rest, square, small = grid_of(y)
    return distance_rows(grid, rest, parts(square, 2), parts(small, 3), soften)


def phase_blocks(y):
    row = row_of(y)
    grid, rest, square, small = grid_of(y)
    product = jnp.sum(jnp.where(row < 3, y * rot(y), 0.0), axis=0, keepdims=True)
    scalars = parts(jnp.where(row == 0, square, jnp.where(row == 1, small, -product)), 3)
    q = [term[0:1] for term in scalars]
    p = [term[1:2] for term in scalars]
    c = [term[2:3] for term in scalars]
    source, target = distance_rows(grid, rest, q, p, cluster_soft)
    y1, y2, y3 = parts(y, 3)
    r1, r2, r3 = rot(y1), rot(y2), rot(y3)
    sources = [
        fill(row, y1, 1.0, c[0]),
        fill(row, y1, 1.0, c[1]),
        fill(row, y2, 1.0, c[2]),
        y2,
        y1,
        y3,
    ]
    targets = [
        fill(row, r1, c[0], 1.0),
        fill(row, r2, c[1], 1.0),
        fill(row, r1, c[2], 1.0),
        r2,
        r3,
        r1,
    ]
    sums = [
        fill(row, y1, 1.0, pltpu.roll(y3, 7, 0)),
        fill(row, y2, pltpu.roll(y3, 2, 0), pltpu.roll(y3, 5, 0)),
    ]
    return (
        jnp.concatenate([source] + sources, axis=0).astype(bf16),
        target.astype(bf16),
        jnp.concatenate(targets, axis=0).astype(bf16),
        jnp.concatenate(sums, axis=0).astype(bf16),
    )


def phase_moment(first, second, y):
    row = row_of(y)
    third = jnp.where(
        row == 0,
        pltpu.roll(first, 1, 0),
        jnp.where(
            row == 1, pltpu.roll(second, 6, 0), jnp.where(row == 2, pltpu.roll(second, 3, 0), 0.0)
        ),
    )
    return first + jnp.where(row == 3, 0.0, second) + third - y * first[3:4]


def mass_rows(y, mass):
    row = row_of(y)
    terms = parts(jnp.where(row < 3, mass * y, jnp.where(row == 3, mass, 0.0)), 3)
    return jnp.concatenate([terms[0] + rot(terms[1]), terms[2]], axis=0).astype(bf16)


def mass_moment(total, y):
    total = total[0:8] + rot(total[0:8]) + total[8:16]
    return jnp.where(row_of(y) < 3, total - y * total[3:4], 0.0)


def mean_of(y):
    mean = jnp.mean(y, axis=1, keepdims=True)
    return jnp.where(row_of(mean) < 3, mean, 0.0)


def weights(sources, targets):
    inverse = lax.rsqrt(dot(sources, targets))
    return inverse * inverse * inverse


def evaluate(y, mass_ref, refs):
    from_ref, to_ref, phase_ref, sum_ref = refs
    n = y.shape[1]
    row = row_of(y)
    y = fill(row, y, 0.0, 0.0)
    source, distance, closing, phase = phase_blocks(y)
    from_ref[...] = source.T
    phase_ref[...] = phase
    ti, tj = block_of(n, 1024), block_of(n, 128)
    for j in range(0, n, tj):
        to_ref[0:48, 2 * j : 2 * j + tj] = distance[:, j : j + tj]
        to_ref[48:96, 2 * j + tj : 2 * j + 2 * tj] = closing[:, j : j + tj]

    def weight_block(across, j):
        both = dot(from_ref[across, :], to_ref[:, pl.ds(2 * j, 2 * tj)])
        inverse = lax.rsqrt(both[:, :tj])
        square = inverse * inverse
        mass = jnp.concatenate([mass_ref[across, :]] * (tj // 128), axis=1)
        weight = square * (inverse * mass)
        radial = weight * square * both[:, tj:]
        return jnp.concatenate(
            [
                jnp.concatenate(split(weight), axis=0),
                jnp.concatenate(split(radial), axis=0),
            ],
            axis=1,
        )

    def sums(across, both):
        phase = phase_ref[:, across]
        return dot(jnp.concatenate([phase, phase], axis=1), both)

    def store(j, total):
        sum_ref[0:16, pl.ds(j, tj)] = total[:, :tj]
        sum_ref[16:32, pl.ds(j, tj)] = total[:, tj:]

    if n == ti:
        every = slice(0, n)
        waiting = None
        for j in range(0, n, tj):
            both = weight_block(every, j)
            if waiting is not None:
                store(j - tj, sums(every, waiting))
            waiting = both
        store(n - tj, sums(every, waiting))
    else:

        def one_block(k, carry):
            j = pl.multiple_of(k * tj, tj)
            total = jnp.zeros((16, 2 * tj), f32)
            for i in range(0, n, ti):
                across = slice(i, i + ti)
                total += sums(across, weight_block(across, j))
            store(j, total)
            return carry

        lax.fori_loop(0, n // tj, one_block, 0)
    direct = phase_moment(sum_ref[0:8, :], sum_ref[8:16, :], y)
    radial = phase_moment(sum_ref[16:24, :], sum_ref[24:32, :], y)
    return direct + jnp.where(row >= 4, 3.0 * rot(radial), 0.0)


def add_up(values):
    while len(values) > 1:
        values = [a + b for a, b in zip(values[::2], values[1::2])]
    return values[0]


def hermite_kernel(pull_count, stars_ref, center_ref, targets_ref, body_rows_ref, *refs):
    pulls, (stars_out, pos_out, vel_out, pull_out, mass_ref, *work) = (
        refs[:pull_count],
        refs[pull_count:],
    )
    own, count = pos_out.shape[1], targets_ref.shape[1]
    stars = stars_ref[...]
    n = stars.shape[1]
    row = row_of(stars)
    mass_ref[...] = jnp.broadcast_to(stars[3:4, :], (128, n)).T
    work[1][...] = jnp.zeros_like(work[1])
    pull = add_up([ref[...] for ref in pulls])
    y = jnp.where(row == 3, 0.0, stars)
    y = y + (step_time / 2.0) * jnp.concatenate([jnp.zeros_like(pull), pull], axis=0)
    frame = jnp.mean(y, axis=1, keepdims=True)
    y = y - frame
    h = step_time / SUBSTEPS
    pos_row, vel_row = row < 3, row >= 4
    guess_vel = jnp.where(pos_row, h, 0.0)
    guess_other = jnp.where(pos_row, h * h * h / 6.0, h)
    kick = jnp.where(vel_row, h / 2.0, 0.0)
    drift = jnp.where(pos_row, h / 2.0, 0.0)
    rates = evaluate(y, mass_ref, work)

    def substep(_, carry):
        y, rates = carry
        vel = rot(y)
        guess = y + guess_vel * vel + (h * h / 2.0) * rates + guess_other * rot(rates)
        fresh = evaluate(guess, mass_ref, work)
        z = y + (h * h / 12.0) * (rates - fresh) + kick * rot(rates + fresh)
        return z + drift * (vel + rot(z)), fresh

    y, _ = lax.fori_loop(0, SUBSTEPS, substep, (y, rates))
    frame = frame + jnp.where(row_of(frame) < 3, step_time * jnp.concatenate([frame[4:8], frame[0:4]], axis=0), 0.0)
    y = y + frame
    stars_out[...] = jnp.where(row == 3, stars, y)
    y = y[:, :own]
    pos_out[...] = y[0:3]
    vel_out[...] = y[4:7]
    y = y - center_ref[:, 0:1]
    source = distance_blocks(y, bridge_soft)[0].astype(bf16).T
    tj = block_of(count, 2048)
    total = jnp.zeros((16, own), f32)
    for j in range(0, count, tj):
        weight = weights(source, targets_ref[:, j : j + tj]).astype(bf16)
        total += dot_t(body_rows_ref[:, j : j + tj], weight)
    pull_out[...] = mass_moment(total, y)[0:3]


def hermite(stars, center, body_targets, body_rows, pulls, own):
    n = stars.shape[1]
    pairs = n * n * (SUBSTEPS + 1)
    return pl.pallas_call(
        functools.partial(hermite_kernel, len(pulls)),
        out_shape=[
            jax.ShapeDtypeStruct(stars.shape, f32),
            jax.ShapeDtypeStruct((3, own), f32),
            jax.ShapeDtypeStruct((3, own), f32),
            jax.ShapeDtypeStruct((3, own), f32),
        ],
        scratch_shapes=[
            pltpu.VMEM((n, 128), f32),
            pltpu.VMEM((n, 96), bf16),
            pltpu.VMEM((96, 2 * n), bf16),
            pltpu.VMEM((16, n), bf16),
            pltpu.VMEM((32, n), f32),
        ],
        compiler_params=pltpu.CompilerParams(vmem_limit_bytes=vmem_limit),
        cost_estimate=pl.CostEstimate(flops=80 * pairs, bytes_accessed=0, transcendentals=pairs),
    )(stars, center, body_targets, body_rows, *pulls)


def sweep(start, stop, step, body):
    if (stop - start) // step <= 8:
        for j in range(start, stop, step):
            body(j)
        return

    def one(k, carry):
        body(pl.multiple_of(start + k * step, step))
        return carry

    lax.fori_loop(0, (stop - start) // step, one, 0)


def kick_kernel(star_own, before, piece_count, *refs):
    pieces, refs = refs[:piece_count], refs[piece_count:]
    held, refs = (refs[:9], refs[9:]) if before else (None, refs)
    outs, (pull_ref, push_ref) = refs[:9], refs[9:]
    center, stars, bodies, source, target, star_rows, body_rows, push, pull = outs
    body_own = pieces[0].shape[2] - star_own
    n, count = stars.shape[1], bodies.shape[1]
    n_held = count_held = 0
    if before:
        n_held, count_held = held[1].shape[1], held[2].shape[1]
        center[...] = held[0][...]
        source[:n_held, :] = held[3][...]
        for old, ref in ((held[1], stars), (held[5], star_rows)):
            ref[:, :n_held] = old[...]
        for old, ref in ((held[2], bodies), (held[4], target), (held[6], body_rows)):
            ref[:, :count_held] = old[...]
    slot = n_held // star_own
    for piece in pieces:
        for k in range(piece.shape[0]):
            stars[:, slot * star_own : (slot + 1) * star_own] = piece[k, :, :star_own]
            bodies[:, slot * body_own : (slot + 1) * body_own] = piece[k, :, star_own:]
            slot += 1
    if not before:
        center[...] = jnp.broadcast_to(mean_of(stars[...]), center.shape)
    middle = center[:, 0:1]
    y = stars[:, n_held:] - middle
    source[n_held:, :] = distance_blocks(y, bridge_soft)[0].astype(bf16).T
    star_rows[:, n_held:] = mass_rows(y, stars[3:4, n_held:])
    x = bodies[:, count_held:] - middle
    target[:, count_held:] = distance_blocks(x, bridge_soft)[1].astype(bf16)
    body_rows[:, count_held:] = mass_rows(x, bodies[3:4, count_held:])
    pull_ref[...] = jnp.zeros_like(pull_ref)
    push_ref[...] = jnp.zeros_like(push_ref)
    tj = block_of(body_own, 256)

    def rectangle(first, last, width, exact, j):
        lanes = pl.ds(j, width)
        ti = block_of(last - first, 1024)
        for i in range(first, last, ti):
            across = slice(i, i + ti)
            high, low = split(weights(source[across, :], target[:, lanes]))
            total = dot(star_rows[:, across], high)
            if exact:
                total += dot(star_rows[:, across], low)
            push_ref[:, lanes] += total
            pull_ref[:, across] += dot_t(body_rows[:, lanes], high)

    def all_pairs(first, last, start, stop, exact):
        if stop > start:
            width = block_of(stop - start, 512)
            sweep(start, stop, width, functools.partial(rectangle, first, last, width, exact))

    if before:
        all_pairs(n_held, n, 0, body_own, True)
        all_pairs(n_held, n, body_own, count_held, False)
        all_pairs(0, n, count_held, count, False)
    else:
        all_pairs(0, n, 0, body_own, True)
        all_pairs(0, n, body_own, count, False)
    total = mass_moment(push_ref[...], bodies[...] - middle)
    push[...] = total
    pull[...] = mass_moment(pull_ref[...], stars[...] - middle)[0:4]
    if before:
        push[:, :count_held] = held[7][...] + total[:, :count_held]
        pull[:, :n_held] = held[8][...] + pull[:, :n_held]


def kick(held, pieces, star_own):
    blocks = sum(piece.shape[0] for piece in pieces)
    body_own = pieces[0].shape[2] - star_own
    new = blocks * blocks
    if held:
        old = held[1].shape[1] // star_own
        new += 2 * old * blocks
        blocks += old
    n, count = blocks * star_own, blocks * body_own
    pairs = new * star_own * body_own
    shapes = [
        ((8, 128), f32),
        ((8, n), f32),
        ((8, count), f32),
        ((n, 48), bf16),
        ((48, count), bf16),
        ((16, n), bf16),
        ((16, count), bf16),
        ((8, count), f32),
        ((4, n), f32),
    ]
    return pl.pallas_call(
        functools.partial(kick_kernel, star_own, bool(held), len(pieces)),
        out_shape=[jax.ShapeDtypeStruct(*shape) for shape in shapes],
        scratch_shapes=[pltpu.VMEM((16, n), f32), pltpu.VMEM((16, count), f32)],
        compiler_params=pltpu.CompilerParams(vmem_limit_bytes=vmem_limit),
        cost_estimate=pl.CostEstimate(flops=40 * pairs, bytes_accessed=0, transcendentals=pairs),
    )(*pieces, *held)


def first_kick(x, axis, star_own):
    pieces = gather_pieces(x, axis)
    held = kick([], pieces[:2], star_own)
    for piece in pieces[2:]:
        held = kick(held, [piece], star_own)
    _, stars, bodies, _, _, _, _, push, pull = held
    return stars, bodies, push, pull


def drift_kernel(bodies_ref, push_ref, pos_out, vel_out, center_out, targets_out, rows_out):
    own = pos_out.shape[1]
    bodies = bodies_ref[...]
    row = row_of(bodies)
    moved = bodies + (step_time / 2.0) * rot(push_ref[...])
    moved = moved + jnp.where(row < 3, step_time * rot(moved), 0.0)
    pos_out[...] = moved[0:3, :own]
    vel_out[...] = moved[4:7, :own]
    middle = mean_of(moved)
    center_out[...] = jnp.broadcast_to(middle, center_out.shape)
    x = moved - middle
    targets_out[...] = distance_blocks(x, bridge_soft)[1].astype(bf16)
    rows_out[...] = mass_rows(x, bodies[3:4, :])


def drift(bodies, push, own):
    count = bodies.shape[1]
    return pl.pallas_call(
        drift_kernel,
        out_shape=[
            jax.ShapeDtypeStruct((3, own), f32),
            jax.ShapeDtypeStruct((3, own), f32),
            jax.ShapeDtypeStruct((8, 128), f32),
            jax.ShapeDtypeStruct((48, count), bf16),
            jax.ShapeDtypeStruct((16, count), bf16),
        ],
        compiler_params=pltpu.CompilerParams(vmem_limit_bytes=vmem_limit),
        cost_estimate=pl.CostEstimate(
            flops=2000 * count, bytes_accessed=200 * count, transcendentals=0
        ),
    )(bodies, push)


def push_kernel(stars_ref, center_ref, targets_ref, pos_ref, vel_ref, vel_out):
    own = vel_out.shape[1]
    stars = stars_ref[...]
    n = stars.shape[1]
    y = stars - center_ref[:, 0:1]
    source = distance_blocks(y, bridge_soft)[0].astype(bf16).T
    star_rows = mass_rows(y, stars[3:4, :])
    ti, tj = block_of(n, 1024), block_of(own, 256)
    for j in range(0, own, tj):
        total = jnp.zeros((16, tj), f32)
        for i in range(0, n, ti):
            high, low = split(weights(source[i : i + ti, :], targets_ref[:, j : j + tj]))
            total += dot(star_rows[:, i : i + ti], high) + dot(star_rows[:, i : i + ti], low)
        x = pos_ref[:, j : j + tj] - center_ref[0:3, 0:1]
        x = jnp.concatenate([x, jnp.zeros((5, tj), f32)], axis=0)
        push = mass_moment(total, x)[0:3]
        vel_out[:, j : j + tj] = vel_ref[:, j : j + tj] + (step_time / 2.0) * push


def second_push(stars, center, targets, pos, vel):
    pairs = stars.shape[1] * pos.shape[1]
    return pl.pallas_call(
        push_kernel,
        grid=(1,),
        in_specs=[
            pl.BlockSpec(stars.shape, lambda i: (0, 0)),
            pl.BlockSpec(center.shape, lambda i: (0, 0)),
            pl.BlockSpec((48, pos.shape[1]), lambda i: (0, 0)),
            pl.BlockSpec(pos.shape, lambda i: (0, 0)),
            pl.BlockSpec(vel.shape, lambda i: (0, 0)),
        ],
        out_specs=pl.BlockSpec(vel.shape, lambda i: (0, 0)),
        out_shape=jax.ShapeDtypeStruct(vel.shape, f32),
        compiler_params=pltpu.CompilerParams(vmem_limit_bytes=vmem_limit),
        cost_estimate=pl.CostEstimate(flops=40 * pairs, bytes_accessed=0, transcendentals=pairs),
    )(stars, center, targets, pos, vel)


def prepare_kernel(
    total_stars, total_bodies, species, pos, vel, mass, body_pos, body_vel, kind, out
):
    own = pos.shape[1]
    out[0:3, :own] = pos[...]
    out[3:4, :own] = mass[...] / total_stars
    out[4:7, :own] = vel[...]
    out[7:8, :] = jnp.zeros_like(out[7:8, :])
    body_mass = jnp.zeros(kind.shape, f32)
    for k in range(species.shape[1]):
        body_mass = body_mass + jnp.where(kind[...] == k, species[:, k : k + 1], 0.0)
    out[0:3, own:] = body_pos[...]
    out[3:4, own:] = body_mass / total_bodies
    out[4:7, own:] = body_vel[...]


def prepare(species, pos, vel, mass, body_pos, body_vel, kind, total_stars, total_bodies):
    whole = pl.BlockSpec(memory_space=pltpu.VMEM)
    return pl.pallas_call(
        functools.partial(prepare_kernel, total_stars, total_bodies),
        in_specs=[whole] * 7,
        out_specs=whole,
        out_shape=jax.ShapeDtypeStruct((8, pos.shape[1] + body_pos.shape[1]), f32),
    )(species[None], pos, vel, mass[None], body_pos, body_vel, kind[None])


def swap(x, axis, bits):
    count = lax.axis_size(axis)
    return lax.ppermute(x, axis, [(i, i ^ bits) for i in range(count)])


def radices(count):
    steps, bit = [], 1
    if count.bit_length() % 2 == 0:
        steps.append((1,))
        bit = 2
    while bit < count:
        steps.append((bit, 2 * bit, 3 * bit))
        bit *= 4
    return steps


def gather_pieces(x, axis):
    pieces = [x[None]]
    for step in radices(lax.axis_size(axis)):
        if len(pieces) > 1:
            pieces = [jnp.concatenate(pieces, axis=0)]
        pieces = pieces + [swap(pieces[0], axis, bits) for bits in step]
    return pieces


def sum_pieces(x, axis):
    pieces = [x]
    for step in radices(lax.axis_size(axis)):
        while len(pieces) > 1:
            pieces = [a + b for a, b in zip(pieces[::2], pieces[1::2])]
        pieces = pieces + [swap(pieces[0], axis, bits) for bits in step]
    return pieces


def local(
    cluster_pos, cluster_vel, cluster_mass, galaxy_pos, galaxy_vel, galaxy_kind, species_mass
):
    own = cluster_pos.shape[1]
    total_stars = own * lax.axis_size("sub")
    total_bodies = galaxy_pos.shape[1] * lax.axis_size("sub") * lax.axis_size("grp")
    block = prepare(
        species_mass,
        cluster_pos,
        cluster_vel,
        cluster_mass,
        galaxy_pos,
        galaxy_vel,
        galaxy_kind,
        total_stars,
        total_bodies,
    )
    stars, bodies, push, pull = first_kick(block, "sub", own)
    pulls = sum_pieces(pull, "grp")
    body_pos, body_vel, center, targets, body_rows = drift(bodies, push, galaxy_pos.shape[1])
    stars, end_pos, end_vel, pull = hermite(stars, center, targets, body_rows, pulls, own)
    pull = add_up(sum_pieces(pull, "grp"))
    body_vel = second_push(stars, center, targets, body_pos, body_vel)
    return end_pos, end_vel + (step_time / 2.0) * pull, body_pos, body_vel


def solution(mesh):
    return jax.shard_map(
        local,
        mesh=mesh,
        in_specs=(
            P(None, "sub"),
            P(None, "sub"),
            P("sub"),
            P(None, ("grp", "sub")),
            P(None, ("grp", "sub")),
            P(("grp", "sub")),
            P(),
        ),
        out_specs=(
            P(None, "sub"),
            P(None, "sub"),
            P(None, ("grp", "sub")),
            P(None, ("grp", "sub")),
        ),
        check_vma=False,
    )
```

time: 431 us -> 55.2 us (0.13)
  blocking collectives: 405 us -> 0 us
  Pallas kernels: 0 us -> 36.9 us
  other arithmetic: 23.9 us -> 1.32 us
  starting transfers between devices: 0 us -> 11.6 us
  waiting for transfers between devices: 0 us -> 4.55 us
    all_gather x11 -> x0, blocking collectives: 328 us -> none  [the longest x9 274 us: evaluate(): source_piece = lax.all_gather(sources, 'sub', axis=1, tiled=True)]
    psum x2 -> x0, blocking collectives: 77.5 us -> none  [kick(): summed = lax.psum(partial_value, ('grp', 'sub'))]
    pallas_call x0 -> x7, Pallas kernels: none -> 36.9 us  [the longest x1 24 us: hermite(): pl.pallas_call(functools.partial(hermite_kernel, len(pulls)), out_shape=[...]
    reduce_sum x27 -> x0, other arithmetic: 18.4 us -> none  [the longest x8 5.29 us: rates_one_tile(): jnp.sum((closing - radial[None] * separation) * weight[None], axis=2)]
    ppermute x0 -> x10, starting transfers between devices: none -> 11.6 us  [swap(): return lax.ppermute(x, axis, [(i, i ^ bits) for i in range(count)])]
    ppermute x0 -> x10, waiting for transfers between devices: none -> 4.55 us  [swap(): return lax.ppermute(x, axis, [(i, i ^ bits) for i in range(count)])]
  transfers between devices with their start and end apart: 0 -> 10, of which waited for: 0 -> 5; matrix products, arithmetic and copies ran while one was open for 0% -> 0% of each run, Pallas kernels for 0% -> 14%
where the time goes in v2:
time: 55.2 us; the launch traced here: 55 us
  Pallas kernels  36.9 us (67%)
  starting transfers between devices  11.6 us (21%)
  waiting for transfers between devices  4.55 us (8%)
  other arithmetic  1.32 us (2%)
  between operations  0.67 us (1%)
    pallas_call x1, Pallas kernels, hermite(): pl.pallas_call(functools.partial(hermite_kernel, len(pulls)), out_shape=[...  24 us
    ppermute x10, starting transfers between devices, swap(): return lax.ppermute(x, axis, [(i, i ^ bits) for i in range(count)])  11.6 us
    pallas_call x3, Pallas kernels, kick(): pl.pallas_call(functools.partial(kick_kernel, star_own, bool(held), len(p...  8.96 us
    ppermute x10, waiting for transfers between devices, swap(): return lax.ppermute(x, axis, [(i, i ^ bits) for i in range(count)])  4.55 us
    pallas_call x1, Pallas kernels, second_push(): pl.pallas_call(push_kernel, grid=(1,), in_specs=[pl.BlockSpec(stars.shape...  1.69 us
    pallas_call x1, Pallas kernels, prepare(): pl.pallas_call(functools.partial(prepare_kernel, total_stars, total_bodie...  1.46 us
  transfers between devices with their start and end apart: 10, of which 5 were waited for; matrix products, arithmetic and copies ran while one was open for 0% of the time, Pallas kernels for 14%

profile of v2, /device:TPU:0, one launch (start us, length us, event | category | flops | bytes accessed | tf_op | source)
XLA Modules:
  0.0 55.0 jit_solution(15860959325898447122)
XLA Ops:
  0.6 1.5 %shard_map.102 = f32[8,640]{1,0:T(8,128)} custom-call(f32[1,4]{1,0:T(1,128)} %bitcast.7, f32[3,128]{1,0:T(4,128)} %pos.1, f32[3,128]{1,0:T(4,128)} %vel.1, f32[1,128]{1,0:T(1,128)} %bitcast.8, f32[3,512]{1,0:T(4,128)} %body_pos.1, f32[3,512]{1,0:T(4,128)} %body_vel.1, s32[1,512]{1,0:T(1,128)} %bitcast.6), custom_call_target="tpu_custom_call" | custom-call | tf_op jit(solution)/shard_map/pallas_call | solution.py:536
  2.1 2.9 %collective-permute-start = (f32[1,8,640]{2,1,0:T(8,128)}, f32[1,8,640]{2,1,0:T(8,128)S(1)}, u32[]{:S(2)}, u32[]{:S(2)}) collective-permute-start(f32[1,8,640]{2,1,0:T(8,128)} %bitcast.4), channel_id=1, source_target_pairs={{0,1},{1,0},{2,3},{3,2},{4,5},{5,4},{6,7},{7,6},{8,9},{9,8},{10,11... | collective-permute-start | bytes 61448 | tf_op jit(solution)/shard_map/ppermute | solution.py:546
  5.0 2.0 %collective-permute-done = f32[1,8,640]{2,1,0:T(8,128)S(1)} collective-permute-done((f32[1,8,640]{2,1,0:T(8,128)}, f32[1,8,640]{2,1,0:T(8,128)S(1)}, u32[]{:S(2)}, u32[]{:S(2)}) %collective-permute-start) | collective-permute-done | bytes 20512 | tf_op jit(solution)/shard_map/ppermute | solution.py:546
  7.0 0.7 %pad_maximum_fusion.refs_0_ = f32[2,8,640]{2,1,0:T(8,128)S(1)} fusion(f32[1,8,640]{2,1,0:T(8,128)S(1)} %collective-permute-done, f32[1,8,640]{2,1,0:T(8,128)} %bitcast.5), kind=kLoop, calls=%fused_computation | loop fusion | flops 10240 | bytes 81920 | tf_op jit(solution)/shard_map/concatenate | solution.py:564
  7.7 2.1 %collective-permute-start.3 = (f32[2,8,640]{2,1,0:T(8,128)S(1)}, f32[2,8,640]{2,1,0:T(8,128)S(1)}, u32[]{:S(2)}, u32[]{:S(2)}) collective-permute-start(f32[2,8,640]{2,1,0:T(8,128)S(1)} %pad_maximum_fusion.refs_0_), channel_id=1, source_target_pairs={{0,2},{1,3},{2,0},{3,1},{4,6},{5,7},{6,4},{7,5},{8,10},{9,11},{10,... | collective-permute-start | bytes 122888 | tf_op jit(solution)/shard_map/ppermute | solution.py:546
  9.8 2.6 %collective-permute-start.2 = (f32[2,8,640]{2,1,0:T(8,128)S(1)}, f32[2,8,640]{2,1,0:T(8,128)S(1)}, u32[]{:S(2)}, u32[]{:S(2)}) collective-permute-start(f32[2,8,640]{2,1,0:T(8,128)S(1)} %pad_maximum_fusion.refs_0_), channel_id=1, source_target_pairs={{0,4},{1,5},{2,6},{3,7},{4,0},{5,1},{6,2},{7,3},{8,12},{9,13},{10,... | collective-permute-start | bytes 122888 | tf_op jit(solution)/shard_map/ppermute | solution.py:546
  12.4 0.0 collective-permute-start.1
  12.4 0.0 collective-permute-done.3.refs_1_
  12.4 2.2 %shard_map.103 = (f32[8,128]{1,0:T(8,128)S(1)}, f32[8,512]{1,0:T(8,128)S(1)}, f32[8,2048]{1,0:T(8,128)S(1)}, bf16[512,48]{1,0:T(8,128)(2,1)S(1)}, bf16[48,2048]{...) custom-call(f32[2,8,640]{2,1,0:T(8,128)S(1)} %pad_maximum_fusion.ref, ...), custom_call_target="tpu_custom_call" | custom-call | flops 41943040 | tf_op jit(solution)/shard_map/pallas_call | solution.py:429
  14.6 1.0 %collective-permute-done.2.refs_0_ = f32[2,8,640]{2,1,0:T(8,128)S(1)} collective-permute-done((f32[2,8,640]{2,1,0:T(8,128)S(1)}, f32[2,8,640]{2,1,0:T(8,128)S(1)}, u32[]{:S(2)}, u32[]{:S(2)}) %collective-permute-start.2) | collective-permute-done | bytes 40992 | tf_op jit(solution)/shard_map/ppermute | solution.py:546
  15.6 2.9 %shard_map.104 = (f32[8,128]{1,0:T(8,128)S(1)}, f32[8,768]{1,0:T(8,128)S(1)}, f32[8,3072]{1,0:T(8,128)S(1)}, bf16[768,48]{1,0:T(8,128)(2,1)S(1)}, bf16[48,3072]{...) custom-call(f32[2,8,640]{2,1,0:T(8,128)S(1)} %collective-permute-don, ...), custom_call_target="tpu_custom_call" | custom-call | flops 52428800 | tf_op jit(solution)/shard_map/pallas_call | solution.py:429
  18.6 0.0 collective-permute-done.1.refs_0_
  18.6 3.8 %shard_map.105 = (f32[8,128]{1,0:T(8,128)}, f32[8,1024]{1,0:T(8,128)S(1)}, f32[8,4096]{1,0:T(8,128)S(1)}, bf16[1024,48]{1,0:T(8,128)(2,1)}, bf16[48,4096]{1,0:T(...) custom-call(f32[2,8,640]{2,1,0:T(8,128)S(1)} %collective-permute-don, ...), custom_call_target="tpu_custom_call" | custom-call | flops 73400320 | tf_op jit(solution)/shard_map/pallas_call | solution.py:429
  22.4 0.0 collective-permute-start.6
  22.4 1.5 %collective-permute-start.5 = (f32[4,1024]{1,0:T(4,128)S(1)}, f32[4,1024]{1,0:T(4,128)S(1)}, u32[]{:S(2)}, u32[]{:S(2)}) collective-permute-start(f32[4,1024]{1,0:T(4,128)S(1)} %get-tuple-element.59.refs_0_), channel_id=1, source_target_pairs={{0,16},{8,24},{16,0},{24,8},{1,17},{9,25},{17,1},{25,9},{2,18},{10... | collective-permute-start | bytes 49160 | tf_op jit(solution)/shard_map/ppermute | solution.py:546
  23.9 0.3 collective-permute-start.4
  24.2 0.7 %shard_map.106 = (f32[3,512]{1,0:T(4,128)}, f32[3,512]{1,0:T(4,128)S(1)}, f32[8,128]{1,0:T(8,128)S(1)}, bf16[48,4096]{1,0:T(8,128)(2,1)S(1)}, bf16[16,4096]{1,0:T(8,128)(2,1)S(1)}) custom-call(f32[8,4096]{1,0:T(8,128)S(1)} %get-tuple-element.54.bodies_ref, f32[8,4096]{1,0:T(8,128)S(1)} %get-tuple-element.55.push_ref), custom_call_target="tpu_custom_call" | custom-call | flops 8192000 | bytes 819200 | tf_op jit(solution)/shard_map/pallas_call | solution.py:464
  25.0 0.7 %collective-permute-done.6.refs_3_ = f32[4,1024]{1,0:T(4,128)S(1)} collective-permute-done((f32[4,1024]{1,0:T(4,128)S(1)}, f32[4,1024]{1,0:T(4,128)S(1)}, u32[]{:S(2)}, u32[]{:S(2)}) %collective-permute-start.6) | collective-permute-done | bytes 16416 | tf_op jit(solution)/shard_map/ppermute | solution.py:546
  25.7 0.5 collective-permute-done.5.refs_2_
  26.2 0.0 collective-permute-done.4.refs_1_
  26.2 0.0 copy-start
  26.2 24.0 %shard_map.107 = (f32[8,1024]{1,0:T(8,128)S(1)}, f32[3,128]{1,0:T(4,128)}, f32[3,128]{1,0:T(4,128)S(1)}, f32[3,128]{1,0:T(4,128)S(1)}) custom-call(f32[8,1024]{1,0:T(8,128)S(1)} %get-tuple-element.53.stars_ref, f32[8,128]{1,0:T(8,128)S(1)} %get-tuple-element.56.center_ref, bf16[48,4096]{1,0:T(8,128)(2,1)S(1)} %get-tuple-element.57.targets_ref, ...), custom_call_target="tpu_custom_call" | custom-call | flops 754974720 | tf_op jit(solution)/shard_map/pallas_call | solution.py:308
  50.2 0.6 %collective-permute-start.9 = (f32[3,128]{1,0:T(4,128)S(1)}, f32[3,128]{1,0:T(4,128)S(1)}, u32[]{:S(2)}, u32[]{:S(2)}) collective-permute-start(f32[3,128]{1,0:T(4,128)S(1)} %get-tuple-element.62), channel_id=1, source_target_pairs={{0,24},{8,16},{16,8},{24,0},{1,25},{9,17},{17,9},{25,1},{2,26},{10... | collective-permute-start | bytes 4616 | tf_op jit(solution)/shard_map/ppermute | solution.py:546
  50.8 1.5 %collective-permute-start.8 = (f32[3,128]{1,0:T(4,128)S(1)}, f32[3,128]{1,0:T(4,128)S(1)}, u32[]{:S(2)}, u32[]{:S(2)}) collective-permute-start(f32[3,128]{1,0:T(4,128)S(1)} %get-tuple-element.62), channel_id=1, source_target_pairs={{0,16},{8,24},{16,0},{24,8},{1,17},{9,25},{17,1},{25,9},{2,18},{10... | collective-permute-start | bytes 4616 | tf_op jit(solution)/shard_map/ppermute | solution.py:546
  52.3 0.0 collective-permute-start.7
  52.3 0.0 copy-done
  52.3 1.7 %shard_map.108 = f32[3,512]{1,0:T(4,128)} custom-call(f32[8,1024]{1,0:T(8,128)S(1)} %get-tuple-element.64.stars_ref, f32[8,128]{1,0:T(8,128)S(1)} %get-tuple-element.56.center_ref, bf16[48,4096]{1,0:T(8,128)(2,1)S(1)} %get-tuple-element.57.targets_ref, f32[3,512]{1,0:T(4,128)S(1)} %copy-done, f32[3,512]{1,0:T(4,128)S(1)} %get-tuple-element.65.vel_ref), custom_call_target="tpu_custom_call" | custom-call | flops 20971520 | tf_op jit(solution)/shard_map/pallas_call | solution.py:501
  54.0 0.0 collective-permute-done.9
  54.0 0.4 collective-permute-done.8
  54.4 0.0 collective-permute-done.7
  54.4 0.6 %multiply_add_fusion = f32[3,128]{1,0:T(4,128)} fusion(f32[3,128]{1,0:T(4,128)S(1)} %get-tuple-element.61, f32[3,128]{1,0:T(4,128)S(1)} %collective-permute-done.8, f32[3,128]{1,0:T(4,128)S(1)} %collective-permute-done.9, f32[3,128]{1,0:T(4,128)S(1)} %get-tuple-element.62, f32[3,128]{1,0:T(4,128)S(1)} %collective-permute-done.7), kind=kLoop, calls=%fused_computation.1 | loop fusion | flops 1920 | bytes 9216 | tf_op jit(solution)/shard_map/add | solution.py:601
Async XLA Ops:
  2.1 4.9 %collective-permute-start = (f32[1,8,640]{2,1,0:T(8,128)}, f32[1,8,640]{2,1,0:T(8,128)S(1)}, u32[]{:S(2)}, u32[]{:S(2)}) collective-permute-start(f32[1,8,640]{2,1,0:T(8,128)} %bitcast.4), channel_id=1, source_target_pairs={{0,1},{1,0},{2,3},{3,2},{4,5},{5,4},{6,7},{7,6},{8,9},{9,8},{10,11... | collective-permute-start | bytes 61448 | tf_op jit(solution)/shard_map/ppermute | solution.py:546
  7.7 4.7 %collective-permute-start.3 = (f32[2,8,640]{2,1,0:T(8,128)S(1)}, f32[2,8,640]{2,1,0:T(8,128)S(1)}, u32[]{:S(2)}, u32[]{:S(2)}) collective-permute-start(f32[2,8,640]{2,1,0:T(8,128)S(1)} %pad_maximum_fusion.refs_0_), channel_id=1, source_target_pairs={{0,2},{1,3},{2,0},{3,1},{4,6},{5,7},{6,4},{7,5},{8,10},{9,11},{10,... | collective-permute-start | bytes 122888 | tf_op jit(solution)/shard_map/ppermute | solution.py:546
  9.8 5.8 %collective-permute-start.2 = (f32[2,8,640]{2,1,0:T(8,128)S(1)}, f32[2,8,640]{2,1,0:T(8,128)S(1)}, u32[]{:S(2)}, u32[]{:S(2)}) collective-permute-start(f32[2,8,640]{2,1,0:T(8,128)S(1)} %pad_maximum_fusion.refs_0_), channel_id=1, source_target_pairs={{0,4},{1,5},{2,6},{3,7},{4,0},{5,1},{6,2},{7,3},{8,12},{9,13},{10,... | collective-permute-start | bytes 122888 | tf_op jit(solution)/shard_map/ppermute | solution.py:546
  12.4 6.1 %collective-permute-start.1 = (f32[2,8,640]{2,1,0:T(8,128)S(1)}, f32[2,8,640]{2,1,0:T(8,128)S(1)}, u32[]{:S(2)}, u32[]{:S(2)}) collective-permute-start(f32[2,8,640]{2,1,0:T(8,128)S(1)} %pad_maximum_fusion.refs_0_), channel_id=1, source_target_pairs={{0,6},{1,7},{2,4},{3,5},{4,2},{5,3},{6,0},{7,1},{8,14},{9,15},{10,... | collective-permute-start | bytes 122888 | tf_op jit(solution)/shard_map/ppermute | solution.py:546
  22.4 3.3 %collective-permute-start.6 = (f32[4,1024]{1,0:T(4,128)S(1)}, f32[4,1024]{1,0:T(4,128)S(1)}, u32[]{:S(2)}, u32[]{:S(2)}) collective-permute-start(f32[4,1024]{1,0:T(4,128)S(1)} %get-tuple-element.59.refs_0_), channel_id=1, source_target_pairs={{0,24},{8,16},{16,8},{24,0},{1,25},{9,17},{17,9},{25,1},{2,26},{10... | collective-permute-start | bytes 49160 | tf_op jit(solution)/shard_map/ppermute | solution.py:546
  22.4 3.8 %collective-permute-start.5 = (f32[4,1024]{1,0:T(4,128)S(1)}, f32[4,1024]{1,0:T(4,128)S(1)}, u32[]{:S(2)}, u32[]{:S(2)}) collective-permute-start(f32[4,1024]{1,0:T(4,128)S(1)} %get-tuple-element.59.refs_0_), channel_id=1, source_target_pairs={{0,16},{8,24},{16,0},{24,8},{1,17},{9,25},{17,1},{25,9},{2,18},{10... | collective-permute-start | bytes 49160 | tf_op jit(solution)/shard_map/ppermute | solution.py:546
  23.9 2.2 %collective-permute-start.4 = (f32[4,1024]{1,0:T(4,128)S(1)}, f32[4,1024]{1,0:T(4,128)S(1)}, u32[]{:S(2)}, u32[]{:S(2)}) collective-permute-start(f32[4,1024]{1,0:T(4,128)S(1)} %get-tuple-element.59.refs_0_), channel_id=1, source_target_pairs={{0,8},{8,0},{16,24},{24,16},{1,9},{9,1},{17,25},{25,17},{2,10},{10... | collective-permute-start | bytes 49160 | tf_op jit(solution)/shard_map/ppermute | solution.py:546
  26.2 26.1 %copy-start = (f32[3,512]{1,0:T(4,128)S(1)}, f32[3,512]{1,0:T(4,128)}, u32[]{:S(2)}) copy-start(f32[3,512]{1,0:T(4,128)} %get-tuple-element.33.pos_ref) | copy-start | bytes 18436
  50.2 3.8 %collective-permute-start.9 = (f32[3,128]{1,0:T(4,128)S(1)}, f32[3,128]{1,0:T(4,128)S(1)}, u32[]{:S(2)}, u32[]{:S(2)}) collective-permute-start(f32[3,128]{1,0:T(4,128)S(1)} %get-tuple-element.62), channel_id=1, source_target_pairs={{0,24},{8,16},{16,8},{24,0},{1,25},{9,17},{17,9},{25,1},{2,26},{10... | collective-permute-start | bytes 4616 | tf_op jit(solution)/shard_map/ppermute | solution.py:546
  50.8 3.6 %collective-permute-start.8 = (f32[3,128]{1,0:T(4,128)S(1)}, f32[3,128]{1,0:T(4,128)S(1)}, u32[]{:S(2)}, u32[]{:S(2)}) collective-permute-start(f32[3,128]{1,0:T(4,128)S(1)} %get-tuple-element.62), channel_id=1, source_target_pairs={{0,16},{8,24},{16,0},{24,8},{1,17},{9,25},{17,1},{25,9},{2,18},{10... | collective-permute-start | bytes 4616 | tf_op jit(solution)/shard_map/ppermute | solution.py:546
  52.3 2.1 %collective-permute-start.7 = (f32[3,128]{1,0:T(4,128)S(1)}, f32[3,128]{1,0:T(4,128)S(1)}, u32[]{:S(2)}, u32[]{:S(2)}) collective-permute-start(f32[3,128]{1,0:T(4,128)S(1)} %get-tuple-element.62), channel_id=1, source_target_pairs={{0,8},{8,0},{16,24},{24,16},{1,9},{9,1},{17,25},{25,17},{2,10},{10... | collective-permute-start | bytes 4616 | tf_op jit(solution)/shard_map/ppermute | solution.py:546

commit v3 on v2

--- a/solution.py
+++ b/solution.py
@@ -338,11 +338,14 @@
     lax.fori_loop(0, (stop - start) // step, one, 0)
 
 
-def kick_kernel(star_own, before, piece_count, *refs):
+def kick_kernel(star_own, before, last, piece_count, *refs):
     pieces, refs = refs[:piece_count], refs[piece_count:]
     held, refs = (refs[:9], refs[9:]) if before else (None, refs)
-    outs, (pull_ref, push_ref) = refs[:9], refs[9:]
-    center, stars, bodies, source, target, star_rows, body_rows, push, pull = outs
+    if last:
+        stars, bodies, push, pull, center, source, target, star_rows, body_rows = refs[:9]
+    else:
+        center, stars, bodies, source, target, star_rows, body_rows, push, pull = refs[:9]
+    pull_ref, push_ref = refs[9:]
     body_own = pieces[0].shape[2] - star_own
     n, count = stars.shape[1], bodies.shape[1]
     n_held = count_held = 0
@@ -405,7 +408,7 @@
         pull[:, :n_held] = held[8][...] + pull[:, :n_held]
 
 
-def kick(held, pieces, star_own):
+def kick(held, pieces, star_own, last):
     blocks = sum(piece.shape[0] for piece in pieces)
     body_own = pieces[0].shape[2] - star_own
     new = blocks * blocks
@@ -426,10 +429,14 @@
         ((8, count), f32),
         ((4, n), f32),
     ]
+    scratch = []
+    if last:
+        scratch = [pltpu.VMEM(*shapes[k]) for k in (0, 3, 4, 5, 6)]
+        shapes = [shapes[k] for k in (1, 2, 7, 8)]
     return pl.pallas_call(
-        functools.partial(kick_kernel, star_own, bool(held), len(pieces)),
+        functools.partial(kick_kernel, star_own, bool(held), last, len(pieces)),
         out_shape=[jax.ShapeDtypeStruct(*shape) for shape in shapes],
-        scratch_shapes=[pltpu.VMEM((16, n), f32), pltpu.VMEM((16, count), f32)],
+        scratch_shapes=scratch + [pltpu.VMEM((16, n), f32), pltpu.VMEM((16, count), f32)],
         compiler_params=pltpu.CompilerParams(vmem_limit_bytes=vmem_limit),
         cost_estimate=pl.CostEstimate(flops=40 * pairs, bytes_accessed=0, transcendentals=pairs),
     )(*pieces, *held)
@@ -437,11 +444,10 @@
 
 def first_kick(x, axis, star_own):
     pieces = gather_pieces(x, axis)
-    held = kick([], pieces[:2], star_own)
-    for piece in pieces[2:]:
-        held = kick(held, [piece], star_own)
-    _, stars, bodies, _, _, _, _, push, pull = held
-    return stars, bodies, push, pull
+    held = kick([], pieces[:2], star_own, len(pieces) <= 2)
+    for k, piece in enumerate(pieces[2:], 3):
+        held = kick(held, [piece], star_own, k == len(pieces))
+    return held
 
 
 def drift_kernel(bodies_ref, push_ref, pos_out, vel_out, center_out, targets_out, rows_out):
@@ -519,25 +525,22 @@
     total_stars, total_bodies, species, pos, vel, mass, body_pos, body_vel, kind, out
 ):
     own = pos.shape[1]
-    out[0:3, :own] = pos[...]
-    out[3:4, :own] = mass[...] / total_stars
-    out[4:7, :own] = vel[...]
-    out[7:8, :] = jnp.zeros_like(out[7:8, :])
+    out[0, 0:3, :own] = pos[...]
+    out[0, 3:4, :own] = mass[...] / total_stars
+    out[0, 4:7, :own] = vel[...]
+    out[0, 7:8, :] = jnp.zeros((1, out.shape[2]), f32)
     body_mass = jnp.zeros(kind.shape, f32)
     for k in range(species.shape[1]):
         body_mass = body_mass + jnp.where(kind[...] == k, species[:, k : k + 1], 0.0)
-    out[0:3, own:] = body_pos[...]
-    out[3:4, own:] = body_mass / total_bodies
-    out[4:7, own:] = body_vel[...]
+    out[0, 0:3, own:] = body_pos[...]
+    out[0, 3:4, own:] = body_mass / total_bodies
+    out[0, 4:7, own:] = body_vel[...]
 
 
 def prepare(species, pos, vel, mass, body_pos, body_vel, kind, total_stars, total_bodies):
-    whole = pl.BlockSpec(memory_space=pltpu.VMEM)
     return pl.pallas_call(
         functools.partial(prepare_kernel, total_stars, total_bodies),
-        in_specs=[whole] * 7,
-        out_specs=whole,
-        out_shape=jax.ShapeDtypeStruct((8, pos.shape[1] + body_pos.shape[1]), f32),
+        out_shape=jax.ShapeDtypeStruct((1, 8, pos.shape[1] + body_pos.shape[1]), f32),
     )(species[None], pos, vel, mass[None], body_pos, body_vel, kind[None])
 
 
@@ -557,12 +560,27 @@
     return steps
 
 
+def copy_kernel(ref, out):
+    out[...] = ref[...]
+
+
+def copy(x):
+    return pl.pallas_call(
+        copy_kernel,
+        out_shape=jax.ShapeDtypeStruct(x.shape, x.dtype),
+        compiler_params=pltpu.CompilerParams(vmem_limit_bytes=vmem_limit),
+    )(x)
+
+
 def gather_pieces(x, axis):
-    pieces = [x[None]]
+    pieces = [x]
     for step in radices(lax.axis_size(axis)):
         if len(pieces) > 1:
             pieces = [jnp.concatenate(pieces, axis=0)]
-        pieces = pieces + [swap(pieces[0], axis, bits) for bits in step]
+        swapped = [swap(pieces[0], axis, bits) for bits in step]
+        if pieces[0] is x:
+            pieces = [copy(x)]
+        pieces = pieces + swapped
     return pieces
 
 

time: 55.2 us -> 53.9 us (0.976)
  waiting for transfers between devices: 4.55 us -> 3.79 us
  local copies, waits for them, and re-layouts: 0.01 us -> 0.76 us
  other arithmetic: 1.32 us -> 0.59 us
  Pallas kernels: 36.9 us -> 36.2 us
    unnamed x2 -> x4, local copies, waits for them, and re-layouts: 0.01 us -> 0.76 us
    ppermute x10, waiting for transfers between devices: 4.55 us -> 3.79 us  [swap(): return lax.ppermute(x, axis, [(i, i ^ bits) for i in range(count)])]
    concatenate x1, other arithmetic: 0.73 us -> 0.01 us  [gather_pieces(): pieces = [jnp.concatenate(pieces, axis=0)]]
    pallas_call x3 -> x4, Pallas kernels: 8.96 us -> 8.32 us  [the longest x3 8.32 us: kick(): pl.pallas_call(functools.partial(kick_kernel, star_own, bool(held), last,...]
where the time goes in v3:
time: 53.9 us; the launch traced here: 53.6 us
  Pallas kernels  36.2 us (67%)
  starting transfers between devices  11.6 us (22%)
  waiting for transfers between devices  3.79 us (7%)
  local copies, waits for them, and re-layouts  0.76 us (1%)
  between operations  0.68 us (1%)
  other arithmetic  0.59 us (1%)
    pallas_call x1, Pallas kernels, hermite(): pl.pallas_call(functools.partial(hermite_kernel, len(pulls)), out_shape=[...  24 us
    ppermute x10, starting transfers between devices, swap(): return lax.ppermute(x, axis, [(i, i ^ bits) for i in range(count)])  11.6 us
    pallas_call x3, Pallas kernels, kick(): pl.pallas_call(functools.partial(kick_kernel, star_own, bool(held), last,...  8.32 us
    ppermute x10, waiting for transfers between devices, swap(): return lax.ppermute(x, axis, [(i, i ^ bits) for i in range(count)])  3.79 us
    pallas_call x1, Pallas kernels, second_push(): pl.pallas_call(push_kernel, grid=(1,), in_specs=[pl.BlockSpec(stars.shape...  1.69 us
    pallas_call x1, Pallas kernels, prepare(): pl.pallas_call(functools.partial(prepare_kernel, total_stars, total_bodie...  1.45 us
  transfers between devices with their start and end apart: 10, of which 5 were waited for; matrix products, arithmetic and copies ran while one was open for 0% of the time, Pallas kernels for 14%

profile of v3, /device:TPU:0, one launch (start us, length us, event | category | flops | bytes accessed | tf_op | source)
XLA Modules:
  0.0 53.6 jit_solution(15910425741065455632)
XLA Ops:
  0.6 1.5 %shard_map.102.ref = f32[1,8,640]{2,1,0:T(8,128)} custom-call(f32[1,4]{1,0:T(1,128)} %bitcast.4, f32[3,128]{1,0:T(4,128)} %pos.1, f32[3,128]{1,0:T(4,128)} %vel.1, f32[1,128]{1,0:T(1,128)} %bitcast.5, f32[3,512]{1,0:T(4,128)} %body_pos.1, f32[3,512]{1,0:T(4,128)} %body_vel.1, s32[1,512]{1,0:T(1,128)} %bitcast.3), custom_call_target="tpu_custom_call" | custom-call | tf_op jit(solution)/shard_map/pallas_call | solution.py:541
  2.1 2.9 %collective-permute-start = (f32[1,8,640]{2,1,0:T(8,128)}, f32[1,8,640]{2,1,0:T(8,128)S(1)}, u32[]{:S(2)}, u32[]{:S(2)}) collective-permute-start(f32[1,8,640]{2,1,0:T(8,128)} %shard_map.102.ref), channel_id=1, source_target_pairs={{0,1},{1,0},{2,3},{3,2},{4,5},{5,4},{6,7},{7,6},{8,9},{9,8},{10,11... | collective-permute-start | bytes 61448 | tf_op jit(solution)/shard_map/ppermute | solution.py:549
  5.0 0.0 copy-start
  5.0 0.8 %copy-done = f32[1,8,640]{2,1,0:T(8,128)S(1)} copy-done((f32[1,8,640]{2,1,0:T(8,128)S(1)}, f32[1,8,640]{2,1,0:T(8,128)}, u32[]{:S(2)}) %copy-start) | copy-done | bytes 20504
  5.8 1.2 %collective-permute-done = f32[1,8,640]{2,1,0:T(8,128)S(1)} collective-permute-done((f32[1,8,640]{2,1,0:T(8,128)}, f32[1,8,640]{2,1,0:T(8,128)S(1)}, u32[]{:S(2)}, u32[]{:S(2)}) %collective-permute-start) | collective-permute-done | bytes 20512 | tf_op jit(solution)/shard_map/ppermute | solution.py:549
  7.0 2.1 %collective-permute-start.3 = (f32[2,8,640]{2,1,0:T(8,128)S(1)}, f32[2,8,640]{2,1,0:T(8,128)S(1)}, u32[]{:S(2)}, u32[]{:S(2)}) collective-permute-start(f32[2,8,640]{2,1,0:T(8,128)S(1)} %pad_maximum_fusion.refs_0_), channel_id=1, source_target_pairs={{0,2},{1,3},{2,0},{3,1},{4,6},{5,7},{6,4},{7,5},{8,10},{9,11},{10,... | collective-permute-start | bytes 122888 | tf_op jit(solution)/shard_map/ppermute | solution.py:549
  9.1 2.6 %collective-permute-start.2 = (f32[2,8,640]{2,1,0:T(8,128)S(1)}, f32[2,8,640]{2,1,0:T(8,128)S(1)}, u32[]{:S(2)}, u32[]{:S(2)}) collective-permute-start(f32[2,8,640]{2,1,0:T(8,128)S(1)} %pad_maximum_fusion.refs_0_), channel_id=1, source_target_pairs={{0,4},{1,5},{2,6},{3,7},{4,0},{5,1},{6,2},{7,3},{8,12},{9,13},{10,... | collective-permute-start | bytes 122888 | tf_op jit(solution)/shard_map/ppermute | solution.py:549
  11.7 0.0 collective-permute-start.1
  11.7 0.0 collective-permute-done.3.refs_1_
  11.7 2.2 %shard_map.104 = (f32[8,128]{1,0:T(8,128)S(1)}, f32[8,512]{1,0:T(8,128)S(1)}, f32[8,2048]{1,0:T(8,128)S(1)}, bf16[512,48]{1,0:T(8,128)(2,1)S(1)}, bf16[48,2048]{...) custom-call(f32[2,8,640]{2,1,0:T(8,128)S(1)} %pad_maximum_fusion.ref, ...), custom_call_target="tpu_custom_call" | custom-call | flops 41943040 | tf_op jit(solution)/shard_map/pallas_call | solution.py:436
  13.9 1.0 %collective-permute-done.2.refs_0_ = f32[2,8,640]{2,1,0:T(8,128)S(1)} collective-permute-done((f32[2,8,640]{2,1,0:T(8,128)S(1)}, f32[2,8,640]{2,1,0:T(8,128)S(1)}, u32[]{:S(2)}, u32[]{:S(2)}) %collective-permute-start.2) | collective-permute-done | bytes 40992 | tf_op jit(solution)/shard_map/ppermute | solution.py:549
  14.9 2.9 %shard_map.105 = (f32[8,128]{1,0:T(8,128)S(1)}, f32[8,768]{1,0:T(8,128)S(1)}, f32[8,3072]{1,0:T(8,128)S(1)}, bf16[768,48]{1,0:T(8,128)(2,1)S(1)}, bf16[48,3072]{...) custom-call(f32[2,8,640]{2,1,0:T(8,128)S(1)} %collective-permute-don, ...), custom_call_target="tpu_custom_call" | custom-call | flops 52428800 | tf_op jit(solution)/shard_map/pallas_call | solution.py:436
  17.8 0.0 collective-permute-done.1.refs_0_
  17.8 3.2 %shard_map.106 = (f32[8,1024]{1,0:T(8,128)S(1)}, f32[8,4096]{1,0:T(8,128)S(1)}, f32[8,4096]{1,0:T(8,128)S(1)}, f32[4,1024]{1,0:T(4,128)S(1)}) custom-call(f32[2,8,640]{2,1,0:T(8,128)S(1)} %collective-permute-done.1.refs_0_, f32[8,128]{1,0:T(8,128)S(1)} %get-tuple-element.44.refs_1_, f32[8,768]{1,0:T(8,128)S(1)} %get-tuple-element.45.refs_2_, ...), custom_call_target="tpu_custom_call" | custom-call | flops 73400320 | tf_op jit(solution)/shard_map/pallas_call | solution.py:436
  21.0 0.1 collective-permute-start.6
  21.1 1.6 %collective-permute-start.5 = (f32[4,1024]{1,0:T(4,128)S(1)}, f32[4,1024]{1,0:T(4,128)S(1)}, u32[]{:S(2)}, u32[]{:S(2)}) collective-permute-start(f32[4,1024]{1,0:T(4,128)S(1)} %get-tuple-element.59.refs_0_), channel_id=1, source_target_pairs={{0,16},{8,24},{16,0},{24,8},{1,17},{9,25},{17,1},{25,9},{2,18},{10... | collective-permute-start | bytes 49160 | tf_op jit(solution)/shard_map/ppermute | solution.py:549
  22.7 0.3 collective-permute-start.4
  22.9 0.7 %shard_map.107 = (f32[3,512]{1,0:T(4,128)}, f32[3,512]{1,0:T(4,128)S(1)}, f32[8,128]{1,0:T(8,128)S(1)}, bf16[48,4096]{1,0:T(8,128)(2,1)S(1)}, bf16[16,4096]{1,0:T(8,128)(2,1)S(1)}) custom-call(f32[8,4096]{1,0:T(8,128)S(1)} %get-tuple-element.54.bodies_ref, f32[8,4096]{1,0:T(8,128)S(1)} %get-tuple-element.55.push_ref), custom_call_target="tpu_custom_call" | custom-call | flops 8192000 | bytes 819200 | tf_op jit(solution)/shard_map/pallas_call | solution.py:470
  23.6 0.7 %collective-permute-done.6.refs_3_ = f32[4,1024]{1,0:T(4,128)S(1)} collective-permute-done((f32[4,1024]{1,0:T(4,128)S(1)}, f32[4,1024]{1,0:T(4,128)S(1)}, u32[]{:S(2)}, u32[]{:S(2)}) %collective-permute-start.6) | collective-permute-done | bytes 16416 | tf_op jit(solution)/shard_map/ppermute | solution.py:549
  24.3 0.6 %collective-permute-done.5.refs_2_ = f32[4,1024]{1,0:T(4,128)S(1)} collective-permute-done((f32[4,1024]{1,0:T(4,128)S(1)}, f32[4,1024]{1,0:T(4,128)S(1)}, u32[]{:S(2)}, u32[]{:S(2)}) %collective-permute-start.5) | collective-permute-done | bytes 16416 | tf_op jit(solution)/shard_map/ppermute | solution.py:549
  24.9 0.0 collective-permute-done.4.refs_1_
  24.9 0.0 copy-start.1
  24.9 24.0 %shard_map.108 = (f32[8,1024]{1,0:T(8,128)S(1)}, f32[3,128]{1,0:T(4,128)}, f32[3,128]{1,0:T(4,128)S(1)}, f32[3,128]{1,0:T(4,128)S(1)}) custom-call(f32[8,1024]{1,0:T(8,128)S(1)} %get-tuple-element.53.stars_ref, f32[8,128]{1,0:T(8,128)S(1)} %get-tuple-element.56.center_ref, bf16[48,4096]{1,0:T(8,128)(2,1)S(1)} %get-tuple-element.57.targets_ref, ...), custom_call_target="tpu_custom_call" | custom-call | flops 754974720 | tf_op jit(solution)/shard_map/pallas_call | solution.py:308
  48.9 0.6 %collective-permute-start.9 = (f32[3,128]{1,0:T(4,128)S(1)}, f32[3,128]{1,0:T(4,128)S(1)}, u32[]{:S(2)}, u32[]{:S(2)}) collective-permute-start(f32[3,128]{1,0:T(4,128)S(1)} %get-tuple-element.62), channel_id=1, source_target_pairs={{0,24},{8,16},{16,8},{24,0},{1,25},{9,17},{17,9},{25,1},{2,26},{10... | collective-permute-start | bytes 4616 | tf_op jit(solution)/shard_map/ppermute | solution.py:549
  49.5 1.5 %collective-permute-start.8 = (f32[3,128]{1,0:T(4,128)S(1)}, f32[3,128]{1,0:T(4,128)S(1)}, u32[]{:S(2)}, u32[]{:S(2)}) collective-permute-start(f32[3,128]{1,0:T(4,128)S(1)} %get-tuple-element.62), channel_id=1, source_target_pairs={{0,16},{8,24},{16,0},{24,8},{1,17},{9,25},{17,1},{25,9},{2,18},{10... | collective-permute-start | bytes 4616 | tf_op jit(solution)/shard_map/ppermute | solution.py:549
  51.0 0.0 collective-permute-start.7
  51.0 0.0 copy-done.1
  51.0 1.7 %shard_map.109 = f32[3,512]{1,0:T(4,128)} custom-call(f32[8,1024]{1,0:T(8,128)S(1)} %get-tuple-element.64.stars_ref, f32[8,128]{1,0:T(8,128)S(1)} %get-tuple-element.56.center_ref, bf16[48,4096]{1,0:T(8,128)(2,1)S(1)} %get-tuple-element.57.targets_ref, f32[3,512]{1,0:T(4,128)S(1)} %copy-done.1, f32[3,512]{1,0:T(4,128)S(1)} %get-tuple-element.65.vel_ref), custom_call_target="tpu_custom_call" | custom-call | flops 20971520 | tf_op jit(solution)/shard_map/pallas_call | solution.py:507
  52.7 0.0 collective-permute-done.9
  52.7 0.4 collective-permute-done.8
  53.1 0.0 collective-permute-done.7
  53.1 0.6 %multiply_add_fusion = f32[3,128]{1,0:T(4,128)} fusion(f32[3,128]{1,0:T(4,128)S(1)} %get-tuple-element.61, f32[3,128]{1,0:T(4,128)S(1)} %collective-permute-done.8, f32[3,128]{1,0:T(4,128)S(1)} %collective-permute-done.9, f32[3,128]{1,0:T(4,128)S(1)} %get-tuple-element.62, f32[3,128]{1,0:T(4,128)S(1)} %collective-permute-done.7), kind=kLoop, calls=%fused_computation.1 | loop fusion | flops 1920 | bytes 9216 | tf_op jit(solution)/shard_map/add | solution.py:619
  (2 shorter events, 0.0 us)
Async XLA Ops:
  2.1 4.9 %collective-permute-start = (f32[1,8,640]{2,1,0:T(8,128)}, f32[1,8,640]{2,1,0:T(8,128)S(1)}, u32[]{:S(2)}, u32[]{:S(2)}) collective-permute-start(f32[1,8,640]{2,1,0:T(8,128)} %shard_map.102.ref), channel_id=1, source_target_pairs={{0,1},{1,0},{2,3},{3,2},{4,5},{5,4},{6,7},{7,6},{8,9},{9,8},{10,11... | collective-permute-start | bytes 61448 | tf_op jit(solution)/shard_map/ppermute | solution.py:549
  5.0 0.8 %copy-start = (f32[1,8,640]{2,1,0:T(8,128)S(1)}, f32[1,8,640]{2,1,0:T(8,128)}, u32[]{:S(2)}) copy-start(f32[1,8,640]{2,1,0:T(8,128)} %shard_map.102.ref) | copy-start | bytes 61444
  7.0 4.7 %collective-permute-start.3 = (f32[2,8,640]{2,1,0:T(8,128)S(1)}, f32[2,8,640]{2,1,0:T(8,128)S(1)}, u32[]{:S(2)}, u32[]{:S(2)}) collective-permute-start(f32[2,8,640]{2,1,0:T(8,128)S(1)} %pad_maximum_fusion.refs_0_), channel_id=1, source_target_pairs={{0,2},{1,3},{2,0},{3,1},{4,6},{5,7},{6,4},{7,5},{8,10},{9,11},{10,... | collective-permute-start | bytes 122888 | tf_op jit(solution)/shard_map/ppermute | solution.py:549
  9.1 5.8 %collective-permute-start.2 = (f32[2,8,640]{2,1,0:T(8,128)S(1)}, f32[2,8,640]{2,1,0:T(8,128)S(1)}, u32[]{:S(2)}, u32[]{:S(2)}) collective-permute-start(f32[2,8,640]{2,1,0:T(8,128)S(1)} %pad_maximum_fusion.refs_0_), channel_id=1, source_target_pairs={{0,4},{1,5},{2,6},{3,7},{4,0},{5,1},{6,2},{7,3},{8,12},{9,13},{10,... | collective-permute-start | bytes 122888 | tf_op jit(solution)/shard_map/ppermute | solution.py:549
  11.7 6.1 %collective-permute-start.1 = (f32[2,8,640]{2,1,0:T(8,128)S(1)}, f32[2,8,640]{2,1,0:T(8,128)S(1)}, u32[]{:S(2)}, u32[]{:S(2)}) collective-permute-start(f32[2,8,640]{2,1,0:T(8,128)S(1)} %pad_maximum_fusion.refs_0_), channel_id=1, source_target_pairs={{0,6},{1,7},{2,4},{3,5},{4,2},{5,3},{6,0},{7,1},{8,14},{9,15},{10,... | collective-permute-start | bytes 122888 | tf_op jit(solution)/shard_map/ppermute | solution.py:549
  21.0 3.3 %collective-permute-start.6 = (f32[4,1024]{1,0:T(4,128)S(1)}, f32[4,1024]{1,0:T(4,128)S(1)}, u32[]{:S(2)}, u32[]{:S(2)}) collective-permute-start(f32[4,1024]{1,0:T(4,128)S(1)} %get-tuple-element.59.refs_0_), channel_id=1, source_target_pairs={{0,24},{8,16},{16,8},{24,0},{1,25},{9,17},{17,9},{25,1},{2,26},{10... | collective-permute-start | bytes 49160 | tf_op jit(solution)/shard_map/ppermute | solution.py:549
  21.1 3.8 %collective-permute-start.5 = (f32[4,1024]{1,0:T(4,128)S(1)}, f32[4,1024]{1,0:T(4,128)S(1)}, u32[]{:S(2)}, u32[]{:S(2)}) collective-permute-start(f32[4,1024]{1,0:T(4,128)S(1)} %get-tuple-element.59.refs_0_), channel_id=1, source_target_pairs={{0,16},{8,24},{16,0},{24,8},{1,17},{9,25},{17,1},{25,9},{2,18},{10... | collective-permute-start | bytes 49160 | tf_op jit(solution)/shard_map/ppermute | solution.py:549
  22.7 2.2 %collective-permute-start.4 = (f32[4,1024]{1,0:T(4,128)S(1)}, f32[4,1024]{1,0:T(4,128)S(1)}, u32[]{:S(2)}, u32[]{:S(2)}) collective-permute-start(f32[4,1024]{1,0:T(4,128)S(1)} %get-tuple-element.59.refs_0_), channel_id=1, source_target_pairs={{0,8},{8,0},{16,24},{24,16},{1,9},{9,1},{17,25},{25,17},{2,10},{10... | collective-permute-start | bytes 49160 | tf_op jit(solution)/shard_map/ppermute | solution.py:549
  24.9 26.1 %copy-start.1 = (f32[3,512]{1,0:T(4,128)S(1)}, f32[3,512]{1,0:T(4,128)}, u32[]{:S(2)}) copy-start(f32[3,512]{1,0:T(4,128)} %get-tuple-element.33.pos_ref) | copy-start | bytes 18436
  48.9 3.8 %collective-permute-start.9 = (f32[3,128]{1,0:T(4,128)S(1)}, f32[3,128]{1,0:T(4,128)S(1)}, u32[]{:S(2)}, u32[]{:S(2)}) collective-permute-start(f32[3,128]{1,0:T(4,128)S(1)} %get-tuple-element.62), channel_id=1, source_target_pairs={{0,24},{8,16},{16,8},{24,0},{1,25},{9,17},{17,9},{25,1},{2,26},{10... | collective-permute-start | bytes 4616 | tf_op jit(solution)/shard_map/ppermute | solution.py:549
  49.5 3.6 %collective-permute-start.8 = (f32[3,128]{1,0:T(4,128)S(1)}, f32[3,128]{1,0:T(4,128)S(1)}, u32[]{:S(2)}, u32[]{:S(2)}) collective-permute-start(f32[3,128]{1,0:T(4,128)S(1)} %get-tuple-element.62), channel_id=1, source_target_pairs={{0,16},{8,24},{16,0},{24,8},{1,17},{9,25},{17,1},{25,9},{2,18},{10... | collective-permute-start | bytes 4616 | tf_op jit(solution)/shard_map/ppermute | solution.py:549
  51.0 2.1 %collective-permute-start.7 = (f32[3,128]{1,0:T(4,128)S(1)}, f32[3,128]{1,0:T(4,128)S(1)}, u32[]{:S(2)}, u32[]{:S(2)}) collective-permute-start(f32[3,128]{1,0:T(4,128)S(1)} %get-tuple-element.62), channel_id=1, source_target_pairs={{0,8},{8,0},{16,24},{24,16},{1,9},{9,1},{17,25},{25,17},{2,10},{10... | collective-permute-start | bytes 4616 | tf_op jit(solution)/shard_map/ppermute | solution.py:549

commit v4 on v3

--- a/solution.py
+++ b/solution.py
@@ -285,7 +285,7 @@
         z = y + (h * h / 12.0) * (rates - fresh) + kick * rot(rates + fresh)
         return z + drift * (vel + rot(z)), fresh
 
-    y, _ = lax.fori_loop(0, SUBSTEPS, substep, (y, rates))
+    y, _ = lax.fori_loop(0, SUBSTEPS, substep, (y, rates), unroll=True)
     frame = frame + jnp.where(row_of(frame) < 3, step_time * jnp.concatenate([frame[4:8], frame[0:4]], axis=0), 0.0)
     y = y + frame
     stars_out[...] = jnp.where(row == 3, stars, y)
@@ -555,7 +555,7 @@
         steps.append((1,))
         bit = 2
     while bit < count:
-        steps.append((bit, 2 * bit, 3 * bit))
+        steps.append((bit, 2 * bit, 3 * bit) if bit == 1 else (2 * bit, bit, 3 * bit))
         bit *= 4
     return steps
 

time: 53.9 us -> 53.3 us (0.989)
  Pallas kernels: 36.2 us -> 35.6 us
    pallas_call x1, Pallas kernels: 24 us -> 23.5 us  [hermite(): pl.pallas_call(functools.partial(hermite_kernel, len(pulls)), out_shape=[...]
  transfers between devices with their start and end apart: 10 -> 10, of which waited for: 5 -> 6; matrix products, arithmetic and copies ran while one was open for 0% -> 0% of each run, Pallas kernels for 14% -> 14%
where the time goes in v4:
time: 53.3 us; the launch traced here: 53 us
  Pallas kernels  35.6 us (67%)
  starting transfers between devices  11.9 us (22%)
  waiting for transfers between devices  3.47 us (7%)
  local copies, waits for them, and re-layouts  0.76 us (1%)
  between operations  0.68 us (1%)
  other arithmetic  0.59 us (1%)
    pallas_call x1, Pallas kernels, hermite(): pl.pallas_call(functools.partial(hermite_kernel, len(pulls)), out_shape=[...  23.5 us
    ppermute x10, starting transfers between devices, swap(): return lax.ppermute(x, axis, [(i, i ^ bits) for i in range(count)])  11.9 us
    pallas_call x3, Pallas kernels, kick(): pl.pallas_call(functools.partial(kick_kernel, star_own, bool(held), last,...  8.31 us
    ppermute x10, waiting for transfers between devices, swap(): return lax.ppermute(x, axis, [(i, i ^ bits) for i in range(count)])  3.47 us
    pallas_call x1, Pallas kernels, second_push(): pl.pallas_call(push_kernel, grid=(1,), in_specs=[pl.BlockSpec(stars.shape...  1.69 us
    pallas_call x1, Pallas kernels, prepare(): pl.pallas_call(functools.partial(prepare_kernel, total_stars, total_bodie...  1.45 us
  transfers between devices with their start and end apart: 10, of which 6 were waited for; matrix products, arithmetic and copies ran while one was open for 0% of the time, Pallas kernels for 14%

profile of v4, /device:TPU:0, one launch (start us, length us, event | category | flops | bytes accessed | tf_op | source)
XLA Modules:
  0.0 53.0 jit_solution(15297149846233076834)
XLA Ops:
  0.6 1.5 %shard_map.102.ref = f32[1,8,640]{2,1,0:T(8,128)} custom-call(f32[1,4]{1,0:T(1,128)} %bitcast.4, f32[3,128]{1,0:T(4,128)} %pos.1, f32[3,128]{1,0:T(4,128)} %vel.1, f32[1,128]{1,0:T(1,128)} %bitcast.5, f32[3,512]{1,0:T(4,128)} %body_pos.1, f32[3,512]{1,0:T(4,128)} %body_vel.1, s32[1,512]{1,0:T(1,128)} %bitcast.3), custom_call_target="tpu_custom_call" | custom-call | tf_op jit(solution)/shard_map/pallas_call | solution.py:541
  2.1 2.9 %collective-permute-start = (f32[1,8,640]{2,1,0:T(8,128)}, f32[1,8,640]{2,1,0:T(8,128)S(1)}, u32[]{:S(2)}, u32[]{:S(2)}) collective-permute-start(f32[1,8,640]{2,1,0:T(8,128)} %shard_map.102.ref), channel_id=1, source_target_pairs={{0,1},{1,0},{2,3},{3,2},{4,5},{5,4},{6,7},{7,6},{8,9},{9,8},{10,11... | collective-permute-start | bytes 61448 | tf_op jit(solution)/shard_map/ppermute | solution.py:549
  5.0 0.0 copy-start
  5.0 0.8 %copy-done = f32[1,8,640]{2,1,0:T(8,128)S(1)} copy-done((f32[1,8,640]{2,1,0:T(8,128)S(1)}, f32[1,8,640]{2,1,0:T(8,128)}, u32[]{:S(2)}) %copy-start) | copy-done | bytes 20504
  5.8 1.2 %collective-permute-done = f32[1,8,640]{2,1,0:T(8,128)S(1)} collective-permute-done((f32[1,8,640]{2,1,0:T(8,128)}, f32[1,8,640]{2,1,0:T(8,128)S(1)}, u32[]{:S(2)}, u32[]{:S(2)}) %collective-permute-start) | collective-permute-done | bytes 20512 | tf_op jit(solution)/shard_map/ppermute | solution.py:549
  7.0 3.1 %collective-permute-start.3 = (f32[2,8,640]{2,1,0:T(8,128)S(1)}, f32[2,8,640]{2,1,0:T(8,128)S(1)}, u32[]{:S(2)}, u32[]{:S(2)}) collective-permute-start(f32[2,8,640]{2,1,0:T(8,128)S(1)} %pad_maximum_fusion.refs_0_), channel_id=1, source_target_pairs={{0,4},{1,5},{2,6},{3,7},{4,0},{5,1},{6,2},{7,3},{8,12},{9,13},{10,... | collective-permute-start | bytes 122888 | tf_op jit(solution)/shard_map/ppermute | solution.py:549
  10.1 1.6 %collective-permute-start.2 = (f32[2,8,640]{2,1,0:T(8,128)S(1)}, f32[2,8,640]{2,1,0:T(8,128)S(1)}, u32[]{:S(2)}, u32[]{:S(2)}) collective-permute-start(f32[2,8,640]{2,1,0:T(8,128)S(1)} %pad_maximum_fusion.refs_0_), channel_id=1, source_target_pairs={{0,2},{1,3},{2,0},{3,1},{4,6},{5,7},{6,4},{7,5},{8,10},{9,11},{10,... | collective-permute-start | bytes 122888 | tf_op jit(solution)/shard_map/ppermute | solution.py:549
  11.7 0.0 collective-permute-start.1
  11.7 0.4 collective-permute-done.3.refs_1_
  12.1 2.2 %shard_map.104 = (f32[8,128]{1,0:T(8,128)S(1)}, f32[8,512]{1,0:T(8,128)S(1)}, f32[8,2048]{1,0:T(8,128)S(1)}, bf16[512,48]{1,0:T(8,128)(2,1)S(1)}, bf16[48,2048]{...) custom-call(f32[2,8,640]{2,1,0:T(8,128)S(1)} %pad_maximum_fusion.ref, ...), custom_call_target="tpu_custom_call" | custom-call | flops 41943040 | tf_op jit(solution)/shard_map/pallas_call | solution.py:436
  14.3 0.0 collective-permute-done.2.refs_0_
  14.3 2.9 %shard_map.105 = (f32[8,128]{1,0:T(8,128)S(1)}, f32[8,768]{1,0:T(8,128)S(1)}, f32[8,3072]{1,0:T(8,128)S(1)}, bf16[768,48]{1,0:T(8,128)(2,1)S(1)}, bf16[48,3072]{...) custom-call(f32[2,8,640]{2,1,0:T(8,128)S(1)} %collective-permute-don, ...), custom_call_target="tpu_custom_call" | custom-call | flops 52428800 | tf_op jit(solution)/shard_map/pallas_call | solution.py:436
  17.3 0.2 collective-permute-done.1.refs_0_
  17.5 3.2 %shard_map.106 = (f32[8,1024]{1,0:T(8,128)S(1)}, f32[8,4096]{1,0:T(8,128)S(1)}, f32[8,4096]{1,0:T(8,128)S(1)}, f32[4,1024]{1,0:T(4,128)S(1)}) custom-call(f32[2,8,640]{2,1,0:T(8,128)S(1)} %collective-permute-done.1.refs_0_, f32[8,128]{1,0:T(8,128)S(1)} %get-tuple-element.44.refs_1_, f32[8,768]{1,0:T(8,128)S(1)} %get-tuple-element.45.refs_2_, ...), custom_call_target="tpu_custom_call" | custom-call | flops 73400320 | tf_op jit(solution)/shard_map/pallas_call | solution.py:436
  20.7 0.1 collective-permute-start.6
  20.7 1.8 %collective-permute-start.5 = (f32[4,1024]{1,0:T(4,128)S(1)}, f32[4,1024]{1,0:T(4,128)S(1)}, u32[]{:S(2)}, u32[]{:S(2)}) collective-permute-start(f32[4,1024]{1,0:T(4,128)S(1)} %get-tuple-element.59.refs_0_), channel_id=1, source_target_pairs={{0,16},{8,24},{16,0},{24,8},{1,17},{9,25},{17,1},{25,9},{2,18},{10... | collective-permute-start | bytes 49160 | tf_op jit(solution)/shard_map/ppermute | solution.py:549
  22.6 0.1 collective-permute-start.4
  22.6 0.7 %shard_map.107 = (f32[3,512]{1,0:T(4,128)}, f32[3,512]{1,0:T(4,128)S(1)}, f32[8,128]{1,0:T(8,128)S(1)}, bf16[48,4096]{1,0:T(8,128)(2,1)S(1)}, bf16[16,4096]{1,0:T(8,128)(2,1)S(1)}) custom-call(f32[8,4096]{1,0:T(8,128)S(1)} %get-tuple-element.54.bodies_ref, f32[8,4096]{1,0:T(8,128)S(1)} %get-tuple-element.55.push_ref), custom_call_target="tpu_custom_call" | custom-call | flops 8192000 | bytes 819200 | tf_op jit(solution)/shard_map/pallas_call | solution.py:470
  23.3 0.5 %collective-permute-done.6.refs_3_ = f32[4,1024]{1,0:T(4,128)S(1)} collective-permute-done((f32[4,1024]{1,0:T(4,128)S(1)}, f32[4,1024]{1,0:T(4,128)S(1)}, u32[]{:S(2)}, u32[]{:S(2)}) %collective-permute-start.6) | collective-permute-done | bytes 16416 | tf_op jit(solution)/shard_map/ppermute | solution.py:549
  23.9 0.7 %collective-permute-done.5.refs_2_ = f32[4,1024]{1,0:T(4,128)S(1)} collective-permute-done((f32[4,1024]{1,0:T(4,128)S(1)}, f32[4,1024]{1,0:T(4,128)S(1)}, u32[]{:S(2)}, u32[]{:S(2)}) %collective-permute-start.5) | collective-permute-done | bytes 16416 | tf_op jit(solution)/shard_map/ppermute | solution.py:549
  24.5 0.0 collective-permute-done.4.refs_1_
  24.5 0.0 copy-start.1
  24.5 23.5 %shard_map.108 = (f32[8,1024]{1,0:T(8,128)S(1)}, f32[3,128]{1,0:T(4,128)}, f32[3,128]{1,0:T(4,128)S(1)}, f32[3,128]{1,0:T(4,128)S(1)}) custom-call(f32[8,1024]{1,0:T(8,128)S(1)} %get-tuple-element.53.stars_ref, f32[8,128]{1,0:T(8,128)S(1)} %get-tuple-element.56.center_ref, bf16[48,4096]{1,0:T(8,128)(2,1)S(1)} %get-tuple-element.57.targets_ref, ...), custom_call_target="tpu_custom_call" | custom-call | flops 754974720 | tf_op jit(solution)/shard_map/pallas_call | solution.py:308
  48.0 0.9 %collective-permute-start.9 = (f32[3,128]{1,0:T(4,128)S(1)}, f32[3,128]{1,0:T(4,128)S(1)}, u32[]{:S(2)}, u32[]{:S(2)}) collective-permute-start(f32[3,128]{1,0:T(4,128)S(1)} %get-tuple-element.62), channel_id=1, source_target_pairs={{0,24},{8,16},{16,8},{24,0},{1,25},{9,17},{17,9},{25,1},{2,26},{10... | collective-permute-start | bytes 4616 | tf_op jit(solution)/shard_map/ppermute | solution.py:549
  48.9 1.4 %collective-permute-start.8 = (f32[3,128]{1,0:T(4,128)S(1)}, f32[3,128]{1,0:T(4,128)S(1)}, u32[]{:S(2)}, u32[]{:S(2)}) collective-permute-start(f32[3,128]{1,0:T(4,128)S(1)} %get-tuple-element.62), channel_id=1, source_target_pairs={{0,16},{8,24},{16,0},{24,8},{1,17},{9,25},{17,1},{25,9},{2,18},{10... | collective-permute-start | bytes 4616 | tf_op jit(solution)/shard_map/ppermute | solution.py:549
  50.3 0.0 collective-permute-start.7
  50.3 0.0 copy-done.1
  50.3 1.7 %shard_map.109 = f32[3,512]{1,0:T(4,128)} custom-call(f32[8,1024]{1,0:T(8,128)S(1)} %get-tuple-element.64.stars_ref, f32[8,128]{1,0:T(8,128)S(1)} %get-tuple-element.56.center_ref, bf16[48,4096]{1,0:T(8,128)(2,1)S(1)} %get-tuple-element.57.targets_ref, f32[3,512]{1,0:T(4,128)S(1)} %copy-done.1, f32[3,512]{1,0:T(4,128)S(1)} %get-tuple-element.65.vel_ref), custom_call_target="tpu_custom_call" | custom-call | flops 20971520 | tf_op jit(solution)/shard_map/pallas_call | solution.py:507
  52.0 0.0 collective-permute-done.9
  52.0 0.4 collective-permute-done.8
  52.4 0.0 collective-permute-done.7
  52.5 0.6 %multiply_add_fusion = f32[3,128]{1,0:T(4,128)} fusion(f32[3,128]{1,0:T(4,128)S(1)} %get-tuple-element.61, f32[3,128]{1,0:T(4,128)S(1)} %collective-permute-done.8, f32[3,128]{1,0:T(4,128)S(1)} %collective-permute-done.9, f32[3,128]{1,0:T(4,128)S(1)} %get-tuple-element.62, f32[3,128]{1,0:T(4,128)S(1)} %collective-permute-done.7), kind=kLoop, calls=%fused_computation.1 | loop fusion | flops 1920 | bytes 9216 | tf_op jit(solution)/shard_map/add | solution.py:619
  (2 shorter events, 0.0 us)
Async XLA Ops:
  2.1 4.9 %collective-permute-start = (f32[1,8,640]{2,1,0:T(8,128)}, f32[1,8,640]{2,1,0:T(8,128)S(1)}, u32[]{:S(2)}, u32[]{:S(2)}) collective-permute-start(f32[1,8,640]{2,1,0:T(8,128)} %shard_map.102.ref), channel_id=1, source_target_pairs={{0,1},{1,0},{2,3},{3,2},{4,5},{5,4},{6,7},{7,6},{8,9},{9,8},{10,11... | collective-permute-start | bytes 61448 | tf_op jit(solution)/shard_map/ppermute | solution.py:549
  5.0 0.8 %copy-start = (f32[1,8,640]{2,1,0:T(8,128)S(1)}, f32[1,8,640]{2,1,0:T(8,128)}, u32[]{:S(2)}) copy-start(f32[1,8,640]{2,1,0:T(8,128)} %shard_map.102.ref) | copy-start | bytes 61444
  7.0 5.1 %collective-permute-start.3 = (f32[2,8,640]{2,1,0:T(8,128)S(1)}, f32[2,8,640]{2,1,0:T(8,128)S(1)}, u32[]{:S(2)}, u32[]{:S(2)}) collective-permute-start(f32[2,8,640]{2,1,0:T(8,128)S(1)} %pad_maximum_fusion.refs_0_), channel_id=1, source_target_pairs={{0,4},{1,5},{2,6},{3,7},{4,0},{5,1},{6,2},{7,3},{8,12},{9,13},{10,... | collective-permute-start | bytes 122888 | tf_op jit(solution)/shard_map/ppermute | solution.py:549
  10.1 4.2 %collective-permute-start.2 = (f32[2,8,640]{2,1,0:T(8,128)S(1)}, f32[2,8,640]{2,1,0:T(8,128)S(1)}, u32[]{:S(2)}, u32[]{:S(2)}) collective-permute-start(f32[2,8,640]{2,1,0:T(8,128)S(1)} %pad_maximum_fusion.refs_0_), channel_id=1, source_target_pairs={{0,2},{1,3},{2,0},{3,1},{4,6},{5,7},{6,4},{7,5},{8,10},{9,11},{10,... | collective-permute-start | bytes 122888 | tf_op jit(solution)/shard_map/ppermute | solution.py:549
  11.7 5.8 %collective-permute-start.1 = (f32[2,8,640]{2,1,0:T(8,128)S(1)}, f32[2,8,640]{2,1,0:T(8,128)S(1)}, u32[]{:S(2)}, u32[]{:S(2)}) collective-permute-start(f32[2,8,640]{2,1,0:T(8,128)S(1)} %pad_maximum_fusion.refs_0_), channel_id=1, source_target_pairs={{0,6},{1,7},{2,4},{3,5},{4,2},{5,3},{6,0},{7,1},{8,14},{9,15},{10,... | collective-permute-start | bytes 122888 | tf_op jit(solution)/shard_map/ppermute | solution.py:549
  20.7 3.2 %collective-permute-start.6 = (f32[4,1024]{1,0:T(4,128)S(1)}, f32[4,1024]{1,0:T(4,128)S(1)}, u32[]{:S(2)}, u32[]{:S(2)}) collective-permute-start(f32[4,1024]{1,0:T(4,128)S(1)} %get-tuple-element.59.refs_0_), channel_id=1, source_target_pairs={{0,24},{8,16},{16,8},{24,0},{1,25},{9,17},{17,9},{25,1},{2,26},{10... | collective-permute-start | bytes 49160 | tf_op jit(solution)/shard_map/ppermute | solution.py:549
  20.7 3.8 %collective-permute-start.5 = (f32[4,1024]{1,0:T(4,128)S(1)}, f32[4,1024]{1,0:T(4,128)S(1)}, u32[]{:S(2)}, u32[]{:S(2)}) collective-permute-start(f32[4,1024]{1,0:T(4,128)S(1)} %get-tuple-element.59.refs_0_), channel_id=1, source_target_pairs={{0,16},{8,24},{16,0},{24,8},{1,17},{9,25},{17,1},{25,9},{2,18},{10... | collective-permute-start | bytes 49160 | tf_op jit(solution)/shard_map/ppermute | solution.py:549
  22.6 2.0 %collective-permute-start.4 = (f32[4,1024]{1,0:T(4,128)S(1)}, f32[4,1024]{1,0:T(4,128)S(1)}, u32[]{:S(2)}, u32[]{:S(2)}) collective-permute-start(f32[4,1024]{1,0:T(4,128)S(1)} %get-tuple-element.59.refs_0_), channel_id=1, source_target_pairs={{0,8},{8,0},{16,24},{24,16},{1,9},{9,1},{17,25},{25,17},{2,10},{10... | collective-permute-start | bytes 49160 | tf_op jit(solution)/shard_map/ppermute | solution.py:549
  24.5 25.8 %copy-start.1 = (f32[3,512]{1,0:T(4,128)S(1)}, f32[3,512]{1,0:T(4,128)}, u32[]{:S(2)}) copy-start(f32[3,512]{1,0:T(4,128)} %get-tuple-element.33.pos_ref) | copy-start | bytes 18436
  48.0 4.0 %collective-permute-start.9 = (f32[3,128]{1,0:T(4,128)S(1)}, f32[3,128]{1,0:T(4,128)S(1)}, u32[]{:S(2)}, u32[]{:S(2)}) collective-permute-start(f32[3,128]{1,0:T(4,128)S(1)} %get-tuple-element.62), channel_id=1, source_target_pairs={{0,24},{8,16},{16,8},{24,0},{1,25},{9,17},{17,9},{25,1},{2,26},{10... | collective-permute-start | bytes 4616 | tf_op jit(solution)/shard_map/ppermute | solution.py:549
  48.9 3.6 %collective-permute-start.8 = (f32[3,128]{1,0:T(4,128)S(1)}, f32[3,128]{1,0:T(4,128)S(1)}, u32[]{:S(2)}, u32[]{:S(2)}) collective-permute-start(f32[3,128]{1,0:T(4,128)S(1)} %get-tuple-element.62), channel_id=1, source_target_pairs={{0,16},{8,24},{16,0},{24,8},{1,17},{9,25},{17,1},{25,9},{2,18},{10... | collective-permute-start | bytes 4616 | tf_op jit(solution)/shard_map/ppermute | solution.py:549
  50.3 2.1 %collective-permute-start.7 = (f32[3,128]{1,0:T(4,128)S(1)}, f32[3,128]{1,0:T(4,128)S(1)}, u32[]{:S(2)}, u32[]{:S(2)}) collective-permute-start(f32[3,128]{1,0:T(4,128)S(1)} %get-tuple-element.62), channel_id=1, source_target_pairs={{0,8},{8,0},{16,24},{24,16},{1,9},{9,1},{17,25},{25,17},{2,10},{10... | collective-permute-start | bytes 4616 | tf_op jit(solution)/shard_map/ppermute | solution.py:549

commit v5 on v4

--- a/solution.py
+++ b/solution.py
@@ -297,8 +297,11 @@
     tj = block_of(count, 2048)
     total = jnp.zeros((16, own), f32)
     for j in range(0, count, tj):
-        weight = weights(source, targets_ref[:, j : j + tj]).astype(bf16)
-        total += dot_t(body_rows_ref[:, j : j + tj], weight)
+        terms = split(weights(source, targets_ref[:, j : j + tj]))
+        moments = body_rows_ref[:, j : j + tj]
+        total += dot_t(
+            jnp.concatenate([moments, moments], axis=1), jnp.concatenate(terms, axis=1)
+        )
     pull_out[...] = mass_moment(total, y)[0:3]
 
 
@@ -374,32 +377,28 @@
     body_rows[:, count_held:] = mass_rows(x, bodies[3:4, count_held:])
     pull_ref[...] = jnp.zeros_like(pull_ref)
     push_ref[...] = jnp.zeros_like(push_ref)
-    tj = block_of(body_own, 256)
-
-    def rectangle(first, last, width, exact, j):
+    def rectangle(first, last, width, j):
         lanes = pl.ds(j, width)
         ti = block_of(last - first, 1024)
+        moments = body_rows[:, lanes]
         for i in range(first, last, ti):
             across = slice(i, i + ti)
-            high, low = split(weights(source[across, :], target[:, lanes]))
-            total = dot(star_rows[:, across], high)
-            if exact:
-                total += dot(star_rows[:, across], low)
-            push_ref[:, lanes] += total
-            pull_ref[:, across] += dot_t(body_rows[:, lanes], high)
-
-    def all_pairs(first, last, start, stop, exact):
-        if stop > start:
-            width = block_of(stop - start, 512)
-            sweep(start, stop, width, functools.partial(rectangle, first, last, width, exact))
+            terms = split(weights(source[across, :], target[:, lanes]))
+            sums = star_rows[:, across]
+            push_ref[:, lanes] += dot(
+                jnp.concatenate([sums, sums], axis=1), jnp.concatenate(terms, axis=0)
+            )
+            pull_ref[:, across] += dot_t(
+                jnp.concatenate([moments, moments], axis=1), jnp.concatenate(terms, axis=1)
+            )
+
+    def all_pairs(first, last, start, stop):
+        width = block_of(stop - start, 512)
+        sweep(start, stop, width, functools.partial(rectangle, first, last, width))
 
     if before:
-        all_pairs(n_held, n, 0, body_own, True)
-        all_pairs(n_held, n, body_own, count_held, False)
-        all_pairs(0, n, count_held, count, False)
-    else:
-        all_pairs(0, n, 0, body_own, True)
-        all_pairs(0, n, body_own, count, False)
+        all_pairs(n_held, n, 0, count_held)
+    all_pairs(0, n, count_held, count)
     total = mass_moment(push_ref[...], bodies[...] - middle)
     push[...] = total
     pull[...] = mass_moment(pull_ref[...], stars[...] - middle)[0:4]

time: 53.3 us -> 56.7 us (1.064)
  Pallas kernels: 35.6 us -> 39.1 us
    pallas_call x3, Pallas kernels: 8.31 us -> 11.6 us  [kick(): pl.pallas_call(functools.partial(kick_kernel, star_own, bool(held), last,...]
  transfers between devices with their start and end apart: 10 -> 10, of which waited for: 6 -> 5; matrix products, arithmetic and copies ran while one was open for 0% -> 0% of each run, Pallas kernels for 14% -> 16%
where the time goes in v5:
time: 56.7 us; the launch traced here: 56.4 us
  Pallas kernels  39.1 us (69%)
  starting transfers between devices  12.2 us (22%)
  waiting for transfers between devices  3.1 us (5%)
  local copies, waits for them, and re-layouts  0.76 us (1%)
  between operations  0.7 us (1%)
  other arithmetic  0.59 us (1%)
    pallas_call x1, Pallas kernels, hermite(): pl.pallas_call(functools.partial(hermite_kernel, len(pulls)), out_shape=[...  23.6 us
    ppermute x10, starting transfers between devices, swap(): return lax.ppermute(x, axis, [(i, i ^ bits) for i in range(count)])  12.2 us
    pallas_call x3, Pallas kernels, kick(): pl.pallas_call(functools.partial(kick_kernel, star_own, bool(held), last,...  11.6 us
    ppermute x10, waiting for transfers between devices, swap(): return lax.ppermute(x, axis, [(i, i ^ bits) for i in range(count)])  3.1 us
    pallas_call x1, Pallas kernels, second_push(): pl.pallas_call(push_kernel, grid=(1,), in_specs=[pl.BlockSpec(stars.shape...  1.69 us
    pallas_call x1, Pallas kernels, prepare(): pl.pallas_call(functools.partial(prepare_kernel, total_stars, total_bodie...  1.45 us
  transfers between devices with their start and end apart: 10, of which 5 were waited for; matrix products, arithmetic and copies ran while one was open for 0% of the time, Pallas kernels for 16%

profile of v5, /device:TPU:0, one launch (start us, length us, event | category | flops | bytes accessed | tf_op | source)
XLA Modules:
  0.0 56.4 jit_solution(5963923271037658381)
XLA Ops:
  0.6 1.5 %shard_map.102.ref = f32[1,8,640]{2,1,0:T(8,128)} custom-call(f32[1,4]{1,0:T(1,128)} %bitcast.4, f32[3,128]{1,0:T(4,128)} %pos.1, f32[3,128]{1,0:T(4,128)} %vel.1, f32[1,128]{1,0:T(1,128)} %bitcast.5, f32[3,512]{1,0:T(4,128)} %body_pos.1, f32[3,512]{1,0:T(4,128)} %body_vel.1, s32[1,512]{1,0:T(1,128)} %bitcast.3), custom_call_target="tpu_custom_call" | custom-call | tf_op jit(solution)/shard_map/pallas_call | solution.py:540
  2.1 2.9 %collective-permute-start = (f32[1,8,640]{2,1,0:T(8,128)}, f32[1,8,640]{2,1,0:T(8,128)S(1)}, u32[]{:S(2)}, u32[]{:S(2)}) collective-permute-start(f32[1,8,640]{2,1,0:T(8,128)} %shard_map.102.ref), channel_id=1, source_target_pairs={{0,1},{1,0},{2,3},{3,2},{4,5},{5,4},{6,7},{7,6},{8,9},{9,8},{10,11... | collective-permute-start | bytes 61448 | tf_op jit(solution)/shard_map/ppermute | solution.py:548
  5.0 0.0 copy-start
  5.0 0.8 %copy-done = f32[1,8,640]{2,1,0:T(8,128)S(1)} copy-done((f32[1,8,640]{2,1,0:T(8,128)S(1)}, f32[1,8,640]{2,1,0:T(8,128)}, u32[]{:S(2)}) %copy-start) | copy-done | bytes 20504
  5.8 1.2 %collective-permute-done = f32[1,8,640]{2,1,0:T(8,128)S(1)} collective-permute-done((f32[1,8,640]{2,1,0:T(8,128)}, f32[1,8,640]{2,1,0:T(8,128)S(1)}, u32[]{:S(2)}, u32[]{:S(2)}) %collective-permute-start) | collective-permute-done | bytes 20512 | tf_op jit(solution)/shard_map/ppermute | solution.py:548
  7.0 3.1 %collective-permute-start.3 = (f32[2,8,640]{2,1,0:T(8,128)S(1)}, f32[2,8,640]{2,1,0:T(8,128)S(1)}, u32[]{:S(2)}, u32[]{:S(2)}) collective-permute-start(f32[2,8,640]{2,1,0:T(8,128)S(1)} %pad_maximum_fusion.refs_0_), channel_id=1, source_target_pairs={{0,4},{1,5},{2,6},{3,7},{4,0},{5,1},{6,2},{7,3},{8,12},{9,13},{10,... | collective-permute-start | bytes 122888 | tf_op jit(solution)/shard_map/ppermute | solution.py:548
  10.1 1.6 %collective-permute-start.2 = (f32[2,8,640]{2,1,0:T(8,128)S(1)}, f32[2,8,640]{2,1,0:T(8,128)S(1)}, u32[]{:S(2)}, u32[]{:S(2)}) collective-permute-start(f32[2,8,640]{2,1,0:T(8,128)S(1)} %pad_maximum_fusion.refs_0_), channel_id=1, source_target_pairs={{0,2},{1,3},{2,0},{3,1},{4,6},{5,7},{6,4},{7,5},{8,10},{9,11},{10,... | collective-permute-start | bytes 122888 | tf_op jit(solution)/shard_map/ppermute | solution.py:548
  11.7 0.0 collective-permute-start.1
  11.7 0.4 collective-permute-done.3.refs_1_
  12.1 2.9 %shard_map.104 = (f32[8,128]{1,0:T(8,128)S(1)}, f32[8,512]{1,0:T(8,128)S(1)}, f32[8,2048]{1,0:T(8,128)S(1)}, bf16[512,48]{1,0:T(8,128)(2,1)S(1)}, bf16[48,2048]{...) custom-call(f32[2,8,640]{2,1,0:T(8,128)S(1)} %pad_maximum_fusion.ref, ...), custom_call_target="tpu_custom_call" | custom-call | flops 41943040 | tf_op jit(solution)/shard_map/pallas_call | solution.py:435
  15.0 0.0 collective-permute-done.2.refs_0_
  15.0 4.0 %shard_map.105 = (f32[8,128]{1,0:T(8,128)S(1)}, f32[8,768]{1,0:T(8,128)S(1)}, f32[8,3072]{1,0:T(8,128)S(1)}, bf16[768,48]{1,0:T(8,128)(2,1)S(1)}, bf16[48,3072]{...) custom-call(f32[2,8,640]{2,1,0:T(8,128)S(1)} %collective-permute-don, ...), custom_call_target="tpu_custom_call" | custom-call | flops 52428800 | tf_op jit(solution)/shard_map/pallas_call | solution.py:435
  19.0 0.0 collective-permute-done.1.refs_0_
  19.0 4.7 %shard_map.106 = (f32[8,1024]{1,0:T(8,128)S(1)}, f32[8,4096]{1,0:T(8,128)S(1)}, f32[8,4096]{1,0:T(8,128)S(1)}, f32[4,1024]{1,0:T(4,128)S(1)}) custom-call(f32[2,8,640]{2,1,0:T(8,128)S(1)} %collective-permute-done.1.refs_0_, f32[8,128]{1,0:T(8,128)S(1)} %get-tuple-element.44.refs_1_, f32[8,768]{1,0:T(8,128)S(1)} %get-tuple-element.45.refs_2_, ...), custom_call_target="tpu_custom_call" | custom-call | flops 73400320 | tf_op jit(solution)/shard_map/pallas_call | solution.py:435
  23.7 0.1 collective-permute-start.6
  23.8 2.0 %collective-permute-start.5 = (f32[4,1024]{1,0:T(4,128)S(1)}, f32[4,1024]{1,0:T(4,128)S(1)}, u32[]{:S(2)}, u32[]{:S(2)}) collective-permute-start(f32[4,1024]{1,0:T(4,128)S(1)} %get-tuple-element.59.refs_0_), channel_id=1, source_target_pairs={{0,16},{8,24},{16,0},{24,8},{1,17},{9,25},{17,1},{25,9},{2,18},{10... | collective-permute-start | bytes 49160 | tf_op jit(solution)/shard_map/ppermute | solution.py:548
  25.9 0.0 collective-permute-start.4
  25.9 0.7 %shard_map.107 = (f32[3,512]{1,0:T(4,128)}, f32[3,512]{1,0:T(4,128)S(1)}, f32[8,128]{1,0:T(8,128)S(1)}, bf16[48,4096]{1,0:T(8,128)(2,1)S(1)}, bf16[16,4096]{1,0:T(8,128)(2,1)S(1)}) custom-call(f32[8,4096]{1,0:T(8,128)S(1)} %get-tuple-element.54.bodies_ref, f32[8,4096]{1,0:T(8,128)S(1)} %get-tuple-element.55.push_ref), custom_call_target="tpu_custom_call" | custom-call | flops 8192000 | bytes 819200 | tf_op jit(solution)/shard_map/pallas_call | solution.py:469
  26.6 0.4 collective-permute-done.6.refs_3_
  27.0 0.7 %collective-permute-done.5.refs_2_ = f32[4,1024]{1,0:T(4,128)S(1)} collective-permute-done((f32[4,1024]{1,0:T(4,128)S(1)}, f32[4,1024]{1,0:T(4,128)S(1)}, u32[]{:S(2)}, u32[]{:S(2)}) %collective-permute-start.5) | collective-permute-done | bytes 16416 | tf_op jit(solution)/shard_map/ppermute | solution.py:548
  27.7 0.0 collective-permute-done.4.refs_1_
  27.7 0.0 copy-start.1
  27.7 23.6 %shard_map.108 = (f32[8,1024]{1,0:T(8,128)S(1)}, f32[3,128]{1,0:T(4,128)}, f32[3,128]{1,0:T(4,128)S(1)}, f32[3,128]{1,0:T(4,128)S(1)}) custom-call(f32[8,1024]{1,0:T(8,128)S(1)} %get-tuple-element.53.stars_ref, f32[8,128]{1,0:T(8,128)S(1)} %get-tuple-element.56.center_ref, bf16[48,4096]{1,0:T(8,128)(2,1)S(1)} %get-tuple-element.57.targets_ref, ...), custom_call_target="tpu_custom_call" | custom-call | flops 754974720 | tf_op jit(solution)/shard_map/pallas_call | solution.py:311
  51.3 1.0 %collective-permute-start.9 = (f32[3,128]{1,0:T(4,128)S(1)}, f32[3,128]{1,0:T(4,128)S(1)}, u32[]{:S(2)}, u32[]{:S(2)}) collective-permute-start(f32[3,128]{1,0:T(4,128)S(1)} %get-tuple-element.62), channel_id=1, source_target_pairs={{0,24},{8,16},{16,8},{24,0},{1,25},{9,17},{17,9},{25,1},{2,26},{10... | collective-permute-start | bytes 4616 | tf_op jit(solution)/shard_map/ppermute | solution.py:548
  52.3 1.5 %collective-permute-start.8 = (f32[3,128]{1,0:T(4,128)S(1)}, f32[3,128]{1,0:T(4,128)S(1)}, u32[]{:S(2)}, u32[]{:S(2)}) collective-permute-start(f32[3,128]{1,0:T(4,128)S(1)} %get-tuple-element.62), channel_id=1, source_target_pairs={{0,16},{8,24},{16,0},{24,8},{1,17},{9,25},{17,1},{25,9},{2,18},{10... | collective-permute-start | bytes 4616 | tf_op jit(solution)/shard_map/ppermute | solution.py:548
  53.7 0.0 collective-permute-start.7
  53.7 0.0 copy-done.1
  53.7 1.7 %shard_map.109 = f32[3,512]{1,0:T(4,128)} custom-call(f32[8,1024]{1,0:T(8,128)S(1)} %get-tuple-element.64.stars_ref, f32[8,128]{1,0:T(8,128)S(1)} %get-tuple-element.56.center_ref, bf16[48,4096]{1,0:T(8,128)(2,1)S(1)} %get-tuple-element.57.targets_ref, f32[3,512]{1,0:T(4,128)S(1)} %copy-done.1, f32[3,512]{1,0:T(4,128)S(1)} %get-tuple-element.65.vel_ref), custom_call_target="tpu_custom_call" | custom-call | flops 20971520 | tf_op jit(solution)/shard_map/pallas_call | solution.py:506
  55.4 0.0 collective-permute-done.9
  55.4 0.4 collective-permute-done.8
  55.9 0.0 collective-permute-done.7
  55.9 0.6 %multiply_add_fusion = f32[3,128]{1,0:T(4,128)} fusion(f32[3,128]{1,0:T(4,128)S(1)} %get-tuple-element.61, f32[3,128]{1,0:T(4,128)S(1)} %collective-permute-done.8, f32[3,128]{1,0:T(4,128)S(1)} %collective-permute-done.9, f32[3,128]{1,0:T(4,128)S(1)} %get-tuple-element.62, f32[3,128]{1,0:T(4,128)S(1)} %collective-permute-done.7), kind=kLoop, calls=%fused_computation.1 | loop fusion | flops 1920 | bytes 9216 | tf_op jit(solution)/shard_map/add | solution.py:618
  (2 shorter events, 0.0 us)
Async XLA Ops:
  2.1 4.9 %collective-permute-start = (f32[1,8,640]{2,1,0:T(8,128)}, f32[1,8,640]{2,1,0:T(8,128)S(1)}, u32[]{:S(2)}, u32[]{:S(2)}) collective-permute-start(f32[1,8,640]{2,1,0:T(8,128)} %shard_map.102.ref), channel_id=1, source_target_pairs={{0,1},{1,0},{2,3},{3,2},{4,5},{5,4},{6,7},{7,6},{8,9},{9,8},{10,11... | collective-permute-start | bytes 61448 | tf_op jit(solution)/shard_map/ppermute | solution.py:548
  5.0 0.8 %copy-start = (f32[1,8,640]{2,1,0:T(8,128)S(1)}, f32[1,8,640]{2,1,0:T(8,128)}, u32[]{:S(2)}) copy-start(f32[1,8,640]{2,1,0:T(8,128)} %shard_map.102.ref) | copy-start | bytes 61444
  7.0 5.1 %collective-permute-start.3 = (f32[2,8,640]{2,1,0:T(8,128)S(1)}, f32[2,8,640]{2,1,0:T(8,128)S(1)}, u32[]{:S(2)}, u32[]{:S(2)}) collective-permute-start(f32[2,8,640]{2,1,0:T(8,128)S(1)} %pad_maximum_fusion.refs_0_), channel_id=1, source_target_pairs={{0,4},{1,5},{2,6},{3,7},{4,0},{5,1},{6,2},{7,3},{8,12},{9,13},{10,... | collective-permute-start | bytes 122888 | tf_op jit(solution)/shard_map/ppermute | solution.py:548
  10.1 4.9 %collective-permute-start.2 = (f32[2,8,640]{2,1,0:T(8,128)S(1)}, f32[2,8,640]{2,1,0:T(8,128)S(1)}, u32[]{:S(2)}, u32[]{:S(2)}) collective-permute-start(f32[2,8,640]{2,1,0:T(8,128)S(1)} %pad_maximum_fusion.refs_0_), channel_id=1, source_target_pairs={{0,2},{1,3},{2,0},{3,1},{4,6},{5,7},{6,4},{7,5},{8,10},{9,11},{10,... | collective-permute-start | bytes 122888 | tf_op jit(solution)/shard_map/ppermute | solution.py:548
  11.7 7.3 %collective-permute-start.1 = (f32[2,8,640]{2,1,0:T(8,128)S(1)}, f32[2,8,640]{2,1,0:T(8,128)S(1)}, u32[]{:S(2)}, u32[]{:S(2)}) collective-permute-start(f32[2,8,640]{2,1,0:T(8,128)S(1)} %pad_maximum_fusion.refs_0_), channel_id=1, source_target_pairs={{0,6},{1,7},{2,4},{3,5},{4,2},{5,3},{6,0},{7,1},{8,14},{9,15},{10,... | collective-permute-start | bytes 122888 | tf_op jit(solution)/shard_map/ppermute | solution.py:548
  23.7 3.2 %collective-permute-start.6 = (f32[4,1024]{1,0:T(4,128)S(1)}, f32[4,1024]{1,0:T(4,128)S(1)}, u32[]{:S(2)}, u32[]{:S(2)}) collective-permute-start(f32[4,1024]{1,0:T(4,128)S(1)} %get-tuple-element.59.refs_0_), channel_id=1, source_target_pairs={{0,24},{8,16},{16,8},{24,0},{1,25},{9,17},{17,9},{25,1},{2,26},{10... | collective-permute-start | bytes 49160 | tf_op jit(solution)/shard_map/ppermute | solution.py:548
  23.8 3.9 %collective-permute-start.5 = (f32[4,1024]{1,0:T(4,128)S(1)}, f32[4,1024]{1,0:T(4,128)S(1)}, u32[]{:S(2)}, u32[]{:S(2)}) collective-permute-start(f32[4,1024]{1,0:T(4,128)S(1)} %get-tuple-element.59.refs_0_), channel_id=1, source_target_pairs={{0,16},{8,24},{16,0},{24,8},{1,17},{9,25},{17,1},{25,9},{2,18},{10... | collective-permute-start | bytes 49160 | tf_op jit(solution)/shard_map/ppermute | solution.py:548
  25.9 1.8 %collective-permute-start.4 = (f32[4,1024]{1,0:T(4,128)S(1)}, f32[4,1024]{1,0:T(4,128)S(1)}, u32[]{:S(2)}, u32[]{:S(2)}) collective-permute-start(f32[4,1024]{1,0:T(4,128)S(1)} %get-tuple-element.59.refs_0_), channel_id=1, source_target_pairs={{0,8},{8,0},{16,24},{24,16},{1,9},{9,1},{17,25},{25,17},{2,10},{10... | collective-permute-start | bytes 49160 | tf_op jit(solution)/shard_map/ppermute | solution.py:548
  27.7 26.1 %copy-start.1 = (f32[3,512]{1,0:T(4,128)S(1)}, f32[3,512]{1,0:T(4,128)}, u32[]{:S(2)}) copy-start(f32[3,512]{1,0:T(4,128)} %get-tuple-element.33.pos_ref) | copy-start | bytes 18436
  51.3 4.1 %collective-permute-start.9 = (f32[3,128]{1,0:T(4,128)S(1)}, f32[3,128]{1,0:T(4,128)S(1)}, u32[]{:S(2)}, u32[]{:S(2)}) collective-permute-start(f32[3,128]{1,0:T(4,128)S(1)} %get-tuple-element.62), channel_id=1, source_target_pairs={{0,24},{8,16},{16,8},{24,0},{1,25},{9,17},{17,9},{25,1},{2,26},{10... | collective-permute-start | bytes 4616 | tf_op jit(solution)/shard_map/ppermute | solution.py:548
  52.3 3.6 %collective-permute-start.8 = (f32[3,128]{1,0:T(4,128)S(1)}, f32[3,128]{1,0:T(4,128)S(1)}, u32[]{:S(2)}, u32[]{:S(2)}) collective-permute-start(f32[3,128]{1,0:T(4,128)S(1)} %get-tuple-element.62), channel_id=1, source_target_pairs={{0,16},{8,24},{16,0},{24,8},{1,17},{9,25},{17,1},{25,9},{2,18},{10... | collective-permute-start | bytes 4616 | tf_op jit(solution)/shard_map/ppermute | solution.py:548
  53.7 2.1 %collective-permute-start.7 = (f32[3,128]{1,0:T(4,128)S(1)}, f32[3,128]{1,0:T(4,128)S(1)}, u32[]{:S(2)}, u32[]{:S(2)}) collective-permute-start(f32[3,128]{1,0:T(4,128)S(1)} %get-tuple-element.62), channel_id=1, source_target_pairs={{0,8},{8,0},{16,24},{24,16},{1,9},{9,1},{17,25},{25,17},{2,10},{10... | collective-permute-start | bytes 4616 | tf_op jit(solution)/shard_map/ppermute | solution.py:548
